TPU v7x, 32 devices: a whole 2x2x4 slice. The times are simulated.
32 devices in a mesh: groups: 2 (over x), grid: 16 (over z, y, core).
Axes of the slice: x: 2, y: 2, z: 4, core: 2. Of those that a mesh axis runs over, the one named last changes fastest.
Arguments:
- values: bfloat16 [128, 64, 1152], P(('groups', 'grid')), parts along dimension 0, may hold values from -4 to 4
- pattern: int32 [64, 18], replicated, may hold values from 0 to 63, as said below
Outputs:
- updated: bfloat16 [128, 64, 1152], P(('groups', 'grid')), parts along dimension 0
- residual: float32 [2], P('groups'), parts along dimension 0
There are 2 independent parts, one for each index of `groups`. A program takes and returns all parts, laid end to end along the dimension named above; an argument that names none is the same for every part. Nothing has to cross between parts.
Inputs may be any that keep to these rules, and one draw needn't show every extreme that they name: `pattern`: block row r is the block at x = r mod 4, y = (r // 4) mod 4, z = r // 16 of a periodic box of 4 x 4 x 4 blocks. Each row lists 18 distinct block columns; the first is the row itself, the others are among the 26 blocks that touch it around the periodic box.
All inputs are finite; a program needn't handle non-finite values.
Results may differ from a plain program's by a relative error of at most 0.0048.
Values may be sent and summed in bfloat16 or wider, within the bound.
A program may use at most 128 MiB of HBM per device.

v0:
```python
import math

import jax
import jax.numpy as jnp
from jax import lax
from jax.sharding import PartitionSpec as P

LAYERS = 4


def passed_along(block, axis, distance):
    devices = range(lax.axis_size(axis))
    route = [((i - distance) % len(devices), i) for i in devices]
    return lax.ppermute(block, axis, route)


def sectioned_window(panel, lines_per_layer, line_y):
    beside = {}
    for offset in (-1, 1, 1 - lines_per_layer, lines_per_layer - 1):
        beside[offset] = passed_along(panel, "grid", -offset)
    below = jnp.where(line_y == 0, beside[lines_per_layer - 1], beside[-1])
    above = jnp.where(line_y == lines_per_layer - 1, beside[1 - lines_per_layer], beside[1])
    stack = jnp.concatenate([below, panel, above], axis=0)
    layered = {}
    for offset in (-lines_per_layer, lines_per_layer):
        layered[offset] = passed_along(stack, "grid", -offset)
    return jnp.concatenate([layered[-lines_per_layer], stack, layered[lines_per_layer]], axis=0)


def touching_window(panel, lines_per_layer, line_y):
    return sectioned_window(panel, lines_per_layer, line_y)


def panel_products(left_panels, window, window_row):
    row_count, block_size, panel_width = left_panels.shape
    slot_count = panel_width // block_size
    tile_view = window.reshape(window.shape[0], block_size, slot_count, block_size)
    slot_index = jnp.arange(slot_count, dtype=jnp.int32)

    def row_product(row_id, row_panel, pattern_rows):
        columns = pattern_rows[row_id]
        neighbour_columns = pattern_rows[columns]
        matches = neighbour_columns[None, :, :] == columns[:, None, None]
        chosen_slot = jnp.sum(jnp.where(matches, slot_index[None, None, :], 0), axis=2)
        present = jnp.any(matches, axis=2)
        local_rows = window_row(columns)
        selected = tile_view[local_rows[None, :], :, chosen_slot, :]
        selected = jnp.where(present[:, :, None, None], selected, jnp.zeros((), window.dtype))
        stacked = selected.reshape(slot_count, slot_count * block_size, block_size)
        product = jnp.einsum("ax,kxc->akc", row_panel, stacked, preferred_element_type=jnp.float32)
        return product.reshape(block_size, slot_count * block_size)

    return row_product


def apply_products(left_panels, row_ids, window, window_row, pattern):
    row_count, block_size, panel_width = left_panels.shape
    row_product = panel_products(left_panels, window, window_row)
    group_size = math.gcd(row_count, 4)
    grouped = lax.map(
        lambda row_batch: jax.vmap(
            lambda one_id, one_panel: row_product(one_id, one_panel, pattern)
        )(row_batch[0], row_batch[1]),
        (
            row_ids.reshape(-1, group_size),
            left_panels.reshape(-1, group_size, block_size, panel_width),
        ),
    )
    return grouped.reshape(row_count, block_size, panel_width)


def identity_panel(block_size, panel_width):
    return jnp.concatenate(
        [
            jnp.eye(block_size, dtype=jnp.float32),
            jnp.zeros((block_size, panel_width - block_size), jnp.float32),
        ],
        axis=1,
    )


def on_device(values, pattern):
    row_count, block_size, panel_width = values.shape
    device_count = lax.axis_size("grid")
    lines_per_layer = device_count // LAYERS
    total_rows = row_count * device_count
    line_index = lax.axis_index("grid")
    line_y = line_index % lines_per_layer
    line_z = line_index // lines_per_layer
    row_ids = line_index * row_count + jnp.arange(row_count, dtype=jnp.int32)

    def window_row(columns):
        line_of = columns // row_count
        place_x = columns % row_count
        step_y = jnp.mod(line_of % lines_per_layer - line_y + 1, lines_per_layer) - 1
        step_z = jnp.mod(line_of // lines_per_layer - line_z + 1, LAYERS) - 1
        return ((step_z + 1) * 3 + step_y + 1) * row_count + place_x

    nearby = touching_window(values, lines_per_layer, line_y)
    square = apply_products(values, row_ids, nearby, window_row, pattern).astype(jnp.bfloat16)
    near_square = touching_window(square, lines_per_layer, line_y)
    product_sum = apply_products(values, row_ids, near_square, window_row, pattern)
    updated = (1.5 * values.astype(jnp.float32) - 0.5 * product_sum).astype(jnp.bfloat16)
    identity = identity_panel(block_size, panel_width)
    deviation = square.astype(jnp.float32) - identity[None]
    local_sum = jnp.sum(deviation * deviation)
    residual = lax.psum(local_sum, "grid") / (total_rows * block_size)
    return (updated, residual.reshape(1))


def solution(mesh):
    in_specs = (P(("groups", "grid"), None, None), P())
    out_specs = (P(("groups", "grid"), None, None), P("groups"))
    return jax.shard_map(
        on_device, mesh=mesh, in_specs=in_specs, out_specs=out_specs, check_vma=False
    )
```

profile of v0, /device:TPU:0, one launch (start us, length us, event | category | flops | bytes accessed | tf_op | source)
XLA Modules:
  0.0 467.2 jit_solution(286457165256563916)
XLA Ops:
  0.6 2.5 collective-permute-start.2
  3.1 3.5 collective-permute-start.3
  6.9 19.1 %collective-permute-done.2 = bf16[4,64,1152]{2,1,0:T(8,128)(2,1)S(1)} collective-permute-done((bf16[4,64,1152]{2,1,0:T(8,128)(2,1)}, bf16[4,64,1152]{2,1,0:T(8,128)(2,1)S(1)}, u32[]{:S(2)}, u32[]{:S(2)}) %collective-permute-start.2) | collective-permute-done | bytes 589856 | tf_op jit(solution)/shard_map/ppermute | solution.py:14
  26.1 5.7 %collective-permute-done = bf16[4,64,1152]{2,1,0:T(8,128)(2,1)S(1)} collective-permute-done((bf16[4,64,1152]{2,1,0:T(8,128)(2,1)}, bf16[4,64,1152]{2,1,0:T(8,128)(2,1)S(1)}, u32[]{:S(2)}, u32[]{:S(2)}) %collective-permute-start) | collective-permute-done | bytes 589856 | tf_op jit(solution)/shard_map/ppermute | solution.py:14
  33.2 2.6 pad_maximum_fusion
  37.8 5.6 %fusion.10 = s32[4,18,18]{0,2,1:T(8,128)S(1)} fusion(s32[4,18]{0,1:T(8,128)S(1)} %copy.36, s32[4,18,18]{2,0,1:T(4,128)S(1)} %copy.35), kind=kLoop, calls=%fused_computation.18 | loop fusion | flops 68688 | bytes 10656 | tf_op jit(solution)/shard_map/while/body/eval_jaxpr/vmap()/reduce_sum | solution.py:44
  43.6 3.5 collective-permute-start.5
  47.3 5.6 %compare_reduce_fusion = pred[4,18,18]{0,2,1:T(8,128)(4,1)S(1)} fusion(s32[4,18]{0,1:T(8,128)S(1)} %copy.36, s32[4,18,18]{2,0,1:T(4,128)S(1)} %copy.35), kind=kLoop, calls=%fused_computation.17 | loop fusion | flops 45360 | bytes 6768 | tf_op jit(solution)/shard_map/while/body/eval_jaxpr/vmap()/reduce_or | solution.py:45
  53.8 25.7 %collective-permute-done.4 = bf16[12,64,1152]{2,1,0:T(8,128)(2,1)} collective-permute-done((bf16[12,64,1152]{2,1,0:T(8,128)(2,1)}, bf16[12,64,1152]{2,1,0:T(8,128)(2,1)}, u32[]{:S(2)}, u32[]{:S(2)}) %collective-permute-start.4) | collective-permute-done | bytes 1769504 | tf_op jit(solution)/shard_map/ppermute | solution.py:14
  79.6 2.8 constant_dynamic-update-slice_fusion.4
  85.0 30.3 %collective-permute-done.5 = bf16[12,64,1152]{2,1,0:T(8,128)(2,1)} collective-permute-done((bf16[12,64,1152]{2,1,0:T(8,128)(2,1)}, bf16[12,64,1152]{2,1,0:T(8,128)(2,1)}, u32[]{:S(2)}, u32[]{:S(2)}) %collective-permute-start.5) | collective-permute-done | bytes 1769504 | tf_op jit(solution)/shard_map/ppermute | solution.py:14
  115.3 2.9 constant_dynamic-update-slice_fusion
  118.2 16.9 %reshape.114 = bf16[36,64,18,64]{3,2,1,0:T(8,128)(2,1)} reshape(bf16[36,64,1152]{2,1,0:T(8,128)(2,1)} %constant_dynamic-update-slice_fusion) | data formatting | bytes 10616832 | tf_op jit(solution)/shard_map/reshape | solution.py:37
  135.1 10.9 %copy.41 = bf16[36,64,18,64]{3,1,2,0:T(8,128)(2,1)} copy(bf16[36,64,18,64]{3,2,1,0:T(8,128)(2,1)} %reshape.114) | data formatting | bytes 10616832 | tf_op jit(solution)/shard_map/reshape | solution.py:37
  146.0 22.9 %gather_fusion.2 = bf16[1296,64,64]{2,1,0:T(8,128)(2,1)} fusion(bf16[36,64,18,64]{3,1,2,0:T(8,128)(2,1)} %copy.41, s32[1296]{0:T(1024)S(1)} %reshape.133), kind=kCustom, calls=%fused_computation.2 | custom fusion | bytes 21244032 | tf_op jit(solution)/shard_map/while/body/eval_jaxpr/vmap()/gather | solution.py:47
  168.9 29.4 %copy.57 = bf16[4,18,1152,64]{2,1,0,3:T(8,128)(2,1)} copy(bf16[4,18,1152,64]{3,2,1,0:T(8,128)(2,1)} %bitcast.33) | data formatting | bytes 21233664 | tf_op jit(solution)/shard_map/while/body/eval_jaxpr/vmap()/gather | solution.py:47
  198.4 10.7 %broadcast_select_fusion.1 = bf16[4,18,1152,64]{2,1,0,3:T(8,128)(2,1)} fusion(bf16[4,18,1152,64]{2,1,0,3:T(8,128)(2,1)} %copy.57, pred[4,18,1152]{2,1,0:T(8,128)(4,1)S(1)} %copy.38), kind=kLoop, calls=%fused_computation.5 | loop fusion | flops 5308416 | bytes 21316608 | tf_op jit(solution)/shard_map/while/body/eval_jaxpr/vmap(jit(_where))/select_n | solution.py:48
  209.1 9.3 %multiply_reduce_fusion = (f32[]{:T(128)}, bf16[4,18,64,64]{3,2,1,0:T(8,128)(2,1)S(1)}) fusion(f32[64,18,64]{0,2,1:T(8,128)S(1)} %bitcast.36, bf16[4,64,1152]{2,1,0:T(8,128)(2,1)S(1)} %copy-done, bf16[4,18,1152,64]{2,1,0,3:T(8,128)(2,1)} %broadcast_select_fusion.1), kind=kOutput, calls=%fused_computation.10 | convolution fusion | flops 680951808 | bytes 12091396 | tf_op jit(solution)/shard_map/while/body/eval_jaxpr/vmap(ax,kxc->akc)/dot_general | solution.py:50
  221.9 2.3 collective-permute-start.9
  224.2 18.9 %collective-permute-done.6 = bf16[4,64,1152]{2,1,0:T(8,128)(2,1)S(1)} collective-permute-done((bf16[4,64,1152]{2,1,0:T(8,128)(2,1)S(1)}, bf16[4,64,1152]{2,1,0:T(8,128)(2,1)S(1)}, u32[]{:S(2)}, u32[]{:S(2)}) %collective-permute-start.6) | collective-permute-done | bytes 589856 | tf_op jit(solution)/shard_map/ppermute | solution.py:14
  243.2 4.1 collective-permute-done.8
  249.6 3.1 collective-permute-start.11
  252.6 100.7 %psum.7 = f32[]{:T(128)} all-reduce(f32[]{:T(128)} %get-tuple-element.38), channel_id=1, replica_groups=mesh['groups'=2,'grid'=16] {'grid'}, use_global_device_ids=true, to_apply=%region_3.4 | all-reduce | flops 1 | bytes 8 | tf_op jit(solution)/shard_map/psum | solution.py:107
  354.0 2.8 constant_dynamic-update-slice_fusion.9
  359.4 2.9 constant_dynamic-update-slice_fusion.5
  362.3 16.9 %reshape.115 = bf16[36,64,18,64]{3,2,1,0:T(8,128)(2,1)} reshape(bf16[36,64,1152]{2,1,0:T(8,128)(2,1)} %constant_dynamic-update-slice_fusion.5) | data formatting | bytes 10616832 | tf_op jit(solution)/shard_map/reshape | solution.py:37
  379.2 10.9 %copy.50 = bf16[36,64,18,64]{3,1,2,0:T(8,128)(2,1)} copy(bf16[36,64,18,64]{3,2,1,0:T(8,128)(2,1)} %reshape.115) | data formatting | bytes 10616832 | tf_op jit(solution)/shard_map/reshape | solution.py:37
  390.1 22.9 %gather_fusion.3 = bf16[1296,64,64]{2,1,0:T(8,128)(2,1)} fusion(bf16[36,64,18,64]{3,1,2,0:T(8,128)(2,1)} %copy.50, s32[1296]{0:T(1024)S(1)} %reshape.133), kind=kCustom, calls=%fused_computation.3 | custom fusion | bytes 21244032 | tf_op jit(solution)/shard_map/while/body/eval_jaxpr/vmap()/gather | solution.py:47
  413.0 29.4 %copy.58 = bf16[4,18,1152,64]{2,1,0,3:T(8,128)(2,1)} copy(bf16[4,18,1152,64]{3,2,1,0:T(8,128)(2,1)} %bitcast.32) | data formatting | bytes 21233664 | tf_op jit(solution)/shard_map/while/body/eval_jaxpr/vmap()/gather | solution.py:47
  442.4 10.7 %broadcast_select_fusion = bf16[4,18,1152,64]{2,1,0,3:T(8,128)(2,1)} fusion(bf16[4,18,1152,64]{2,1,0,3:T(8,128)(2,1)} %copy.58, pred[4,18,1152]{2,1,0:T(8,128)(4,1)S(1)} %copy.38), kind=kLoop, calls=%fused_computation.4 | loop fusion | flops 5308416 | bytes 21316608 | tf_op jit(solution)/shard_map/while/body/eval_jaxpr/vmap(jit(_where))/select_n | solution.py:48
  453.1 9.9 %fusion.4 = f32[4,18,64,64]{3,2,1,0:T(8,128)} fusion(bf16[4,18,1152,64]{2,1,0,3:T(8,128)(2,1)} %broadcast_select_fusion, bf16[4,64,1152]{2,1,0:T(8,128)(2,1)S(1)} %copy-done), kind=kOutput, calls=%fused_computation.13 | convolution fusion | flops 679772160 | bytes 12386304 | tf_op jit(solution)/shard_map/while/body/eval_jaxpr/vmap(ax,kxc->akc)/dot_general | solution.py:50
  463.0 2.0 copy.53
  (51 shorter events, 17.1 us)
Async XLA Ops:
  0.6 35.6 %copy-start.1 = (s32[64,18]{0,1:T(8,128)S(1)}, s32[64,18]{0,1:T(8,128)}, u32[]{:S(2)}) copy-start(s32[64,18]{0,1:T(8,128)} %param.3) | copy-start | bytes 13828
  0.6 25.4 %collective-permute-start.2 = (bf16[4,64,1152]{2,1,0:T(8,128)(2,1)}, bf16[4,64,1152]{2,1,0:T(8,128)(2,1)S(1)}, u32[]{:S(2)}, u32[]{:S(2)}) collective-permute-start(bf16[4,64,1152]{2,1,0:T(8,128)(2,1)} %param.2), channel_id=1, source_target_pairs={{13,0},{14,1},{15,2},{0,3},{1,4},{2,5},{3,6},{4,7},{5,8},{6,9},{7,... | collective-permute-start | bytes 1769480 | tf_op jit(solution)/shard_map/ppermute | solution.py:14
  3.1 22.9 %collective-permute-start.3 = (bf16[4,64,1152]{2,1,0:T(8,128)(2,1)}, bf16[4,64,1152]{2,1,0:T(8,128)(2,1)S(1)}, u32[]{:S(2)}, u32[]{:S(2)}) collective-permute-start(bf16[4,64,1152]{2,1,0:T(8,128)(2,1)} %param.2), channel_id=1, source_target_pairs={{1,0},{2,1},{3,2},{4,3},{5,4},{6,5},{7,6},{8,7},{9,8},{10,9},{11,1... | collective-permute-start | bytes 1769480 | tf_op jit(solution)/shard_map/ppermute | solution.py:14
  6.6 25.2 %collective-permute-start = (bf16[4,64,1152]{2,1,0:T(8,128)(2,1)}, bf16[4,64,1152]{2,1,0:T(8,128)(2,1)S(1)}, u32[]{:S(2)}, u32[]{:S(2)}) collective-permute-start(bf16[4,64,1152]{2,1,0:T(8,128)(2,1)} %param.2), channel_id=1, source_target_pairs={{3,0},{4,1},{5,2},{6,3},{7,4},{8,5},{9,6},{10,7},{11,8},{12,9},{13... | collective-permute-start | bytes 1769480 | tf_op jit(solution)/shard_map/ppermute | solution.py:14
  6.8 26.3 %collective-permute-start.1 = (bf16[4,64,1152]{2,1,0:T(8,128)(2,1)}, bf16[4,64,1152]{2,1,0:T(8,128)(2,1)S(1)}, u32[]{:S(2)}, u32[]{:S(2)}) collective-permute-start(bf16[4,64,1152]{2,1,0:T(8,128)(2,1)} %param.2), channel_id=1, source_target_pairs={{15,0},{0,1},{1,2},{2,3},{3,4},{4,5},{5,6},{6,7},{7,8},{8,9},{9,10... | collective-permute-start | bytes 1769480 | tf_op jit(solution)/shard_map/ppermute | solution.py:14
  33.2 50.0 %copy-start = (bf16[4,64,1152]{2,1,0:T(8,128)(2,1)S(1)}, bf16[4,64,1152]{2,1,0:T(8,128)(2,1)}, u32[]{:S(2)}) copy-start(bf16[4,64,1152]{2,1,0:T(8,128)(2,1)} %param.2) | copy-start | bytes 1769476
  35.8 43.7 %collective-permute-start.4 = (bf16[12,64,1152]{2,1,0:T(8,128)(2,1)}, bf16[12,64,1152]{2,1,0:T(8,128)(2,1)}, u32[]{:S(2)}, u32[]{:S(2)}) collective-permute-start(bf16[12,64,1152]{2,1,0:T(8,128)(2,1)} %pad_maximum_fusion), channel_id=1, source_target_pairs={{12,0},{13,1},{14,2},{15,3},{0,4},{1,5},{2,6},{3,7},{4,8},{5,9},{6... | collective-permute-start | bytes 5308424 | tf_op jit(solution)/shard_map/ppermute | solution.py:14
  43.6 71.7 %collective-permute-start.5 = (bf16[12,64,1152]{2,1,0:T(8,128)(2,1)}, bf16[12,64,1152]{2,1,0:T(8,128)(2,1)}, u32[]{:S(2)}, u32[]{:S(2)}) collective-permute-start(bf16[12,64,1152]{2,1,0:T(8,128)(2,1)} %pad_maximum_fusion), channel_id=1, source_target_pairs={{4,0},{5,1},{6,2},{7,3},{8,4},{9,5},{10,6},{11,7},{12,8},{13,9},{1... | collective-permute-start | bytes 5308424 | tf_op jit(solution)/shard_map/ppermute | solution.py:14
  219.0 24.1 %collective-permute-start.6 = (bf16[4,64,1152]{2,1,0:T(8,128)(2,1)S(1)}, bf16[4,64,1152]{2,1,0:T(8,128)(2,1)S(1)}, u32[]{:S(2)}, u32[]{:S(2)}) collective-permute-start(bf16[4,64,1152]{2,1,0:T(8,128)(2,1)S(1)} %copy.44), channel_id=1, source_target_pairs={{3,0},{4,1},{5,2},{6,3},{7,4},{8,5},{9,6},{10,7},{11,8},{12,9},{13... | collective-permute-start | bytes 1769480 | tf_op jit(solution)/shard_map/ppermute | solution.py:14
  219.1 24.0 %collective-permute-start.7 = (bf16[4,64,1152]{2,1,0:T(8,128)(2,1)S(1)}, bf16[4,64,1152]{2,1,0:T(8,128)(2,1)S(1)}, u32[]{:S(2)}, u32[]{:S(2)}) collective-permute-start(bf16[4,64,1152]{2,1,0:T(8,128)(2,1)S(1)} %copy.44), channel_id=1, source_target_pairs={{15,0},{0,1},{1,2},{2,3},{3,4},{4,5},{5,6},{6,7},{7,8},{8,9},{9,10... | collective-permute-start | bytes 1769480 | tf_op jit(solution)/shard_map/ppermute | solution.py:14
  220.8 26.4 %collective-permute-start.8 = (bf16[4,64,1152]{2,1,0:T(8,128)(2,1)S(1)}, bf16[4,64,1152]{2,1,0:T(8,128)(2,1)S(1)}, u32[]{:S(2)}, u32[]{:S(2)}) collective-permute-start(bf16[4,64,1152]{2,1,0:T(8,128)(2,1)S(1)} %copy.44), channel_id=1, source_target_pairs={{13,0},{14,1},{15,2},{0,3},{1,4},{2,5},{3,6},{4,7},{5,8},{6,9},{7,... | collective-permute-start | bytes 1769480 | tf_op jit(solution)/shard_map/ppermute | solution.py:14
  221.9 25.4 %collective-permute-start.9 = (bf16[4,64,1152]{2,1,0:T(8,128)(2,1)S(1)}, bf16[4,64,1152]{2,1,0:T(8,128)(2,1)S(1)}, u32[]{:S(2)}, u32[]{:S(2)}) collective-permute-start(bf16[4,64,1152]{2,1,0:T(8,128)(2,1)S(1)} %copy.44), channel_id=1, source_target_pairs={{1,0},{2,1},{3,2},{4,3},{5,4},{6,5},{7,6},{8,7},{9,8},{10,9},{11,1... | collective-permute-start | bytes 1769480 | tf_op jit(solution)/shard_map/ppermute | solution.py:14
  248.8 105.1 %collective-permute-start.10 = (bf16[12,64,1152]{2,1,0:T(8,128)(2,1)}, bf16[12,64,1152]{2,1,0:T(8,128)(2,1)}, u32[]{:S(2)}, u32[]{:S(2)}) collective-permute-start(bf16[12,64,1152]{2,1,0:T(8,128)(2,1)} %pad_maximum_fusion.1), channel_id=1, source_target_pairs={{12,0},{13,1},{14,2},{15,3},{0,4},{1,5},{2,6},{3,7},{4,8},{5,9},{6... | collective-permute-start | bytes 5308424 | tf_op jit(solution)/shard_map/ppermute | solution.py:14
  249.6 109.9 %collective-permute-start.11 = (bf16[12,64,1152]{2,1,0:T(8,128)(2,1)}, bf16[12,64,1152]{2,1,0:T(8,128)(2,1)}, u32[]{:S(2)}, u32[]{:S(2)}) collective-permute-start(bf16[12,64,1152]{2,1,0:T(8,128)(2,1)} %pad_maximum_fusion.1), channel_id=1, source_target_pairs={{4,0},{5,1},{6,2},{7,3},{8,4},{9,5},{10,6},{11,7},{12,8},{13,9},{1... | collective-permute-start | bytes 5308424 | tf_op jit(solution)/shard_map/ppermute | solution.py:14
where the time goes:
time: 470 us; the launch traced here: 467 us
  local copies, waits for them, and re-layouts  182 us (39%)
  waiting for transfers between devices  105 us (22%)
  blocking collectives  101 us (21%)
  other arithmetic  38.1 us (8%)
  matrix products  19.3 us (4%)
  starting transfers between devices  19.2 us (4%)
    ppermute x12, waiting for transfers between devices, passed_along(): return lax.ppermute(block, axis, route)  105 us
    gather x4, local copies, waits for them, and re-layouts, row_product(): selected = tile_view[local_rows[None, :], :, chosen_slot, :]  105 us
    psum x1, blocking collectives, on_device(): residual = lax.psum(local_sum, 'grid') / (total_rows * block_size)  101 us
    reshape x4, local copies, waits for them, and re-layouts, panel_products(): window.reshape(window.shape[0], block_size, slot_count, block_size)  55.6 us
    select_n x2, other arithmetic, row_product(): jnp.where(present[:, :, None, None], selected, jnp.zeros((), window.dtype))  21.4 us
    dot_general x2, matrix products, row_product(): jnp.einsum('ax,kxc->akc', row_panel, stacked, preferred_element_type=jnp....  19.3 us
    ppermute x12, starting transfers between devices, passed_along(): return lax.ppermute(block, axis, route)  19.2 us
    unnamed x13, local copies, waits for them, and re-layouts  11 us
  transfers between devices with their start and end apart: 12, of which 7 were waited for; matrix products, arithmetic and copies ran while one was open for 5% of the time, Pallas kernels for 0%

commit v1 on v0

v1 whole, which is shorter than its diff:
```python
import functools

import jax
import jax.numpy as jnp
from jax import lax
from jax.experimental import pallas as pl
from jax.experimental.pallas import tpu as pltpu
from jax.sharding import PartitionSpec as P

LAYERS = 4
MESH = pl.DeviceIdType.MESH


def tile_tables(pattern, line_index, lines_per_layer, row_count, block_size):
    slot_count = pattern.shape[1]
    line_y = line_index % lines_per_layer
    line_z = line_index // lines_per_layer
    columns = lax.dynamic_slice(pattern, (line_index * row_count, 0), (row_count, slot_count))
    line_of = columns // row_count
    place_x = columns % row_count
    step_y = jnp.mod(line_of % lines_per_layer - line_y + 1, lines_per_layer) - 1
    step_z = jnp.mod(line_of // lines_per_layer - line_z + 1, LAYERS) - 1
    place = ((step_z + 1) * 3 + step_y + 1) * row_count + place_x
    places = 9 * row_count
    matches = place[:, None, :] == jnp.arange(places, dtype=jnp.int32)[None, :, None]
    slots = jnp.arange(slot_count, dtype=jnp.int32) + 1
    slot_at = jnp.sum(jnp.where(matches, slots, 0), axis=2) - 1
    stored = (slot_at >= 0).astype(jnp.float32)
    mask = jnp.repeat(stored.reshape(row_count, 9, row_count), block_size, axis=2)
    return place.reshape(-1), slot_at.reshape(-1), mask.transpose(1, 0, 2)


def swapped(tile):
    return pltpu.roll(tile, tile.shape[1] // 2, 1)


def low_half(block):
    return lax.broadcasted_iota(jnp.int32, (block, 2 * block), 1) < block


def expand_kernel(slot_ref, v_ref, dense):
    row_count, block, width = v_ref.shape
    places = 9 * row_count
    pair = 2 * block
    low = low_half(block)

    def expand(c, carry):
        for x in range(row_count):
            rows = pl.ds(x * block, block)
            for h in range(row_count // 2):
                parts = []
                for side in range(2):
                    slot = slot_ref[x * places + c * row_count + 2 * h + side]
                    known = jnp.maximum(slot, 0)
                    at = pl.multiple_of((known >> 1) * pair, pair)
                    tile = v_ref[x, :, pl.ds(at, pair)].astype(jnp.float32)
                    tile = jnp.where((known & 1) == side, tile, swapped(tile))
                    parts.append(jnp.where(slot >= 0, tile, 0.0))
                both = jnp.where(low, parts[0], parts[1])
                dense[c // 3, c % 3, rows, pl.ds(h * pair, pair)] = both.astype(jnp.bfloat16)
        return carry

    lax.fori_loop(0, 9, expand, 0)


def compact_kernel(place_ref, total, v_ref, out_ref):
    row_count, block, width = v_ref.shape
    slot_count = width // block
    pair = 2 * block
    low = low_half(block)

    def compact(k, carry):
        at = pl.multiple_of(k * pair, pair)
        for x in range(row_count):
            rows = pl.ds(x * block, block)
            parts = []
            for side in range(2):
                place = place_ref[x * slot_count + 2 * k + side]
                tile = total[place >> 1, rows, :]
                parts.append(jnp.where((place & 1) == side, tile, swapped(tile)))
            both = jnp.where(low, parts[0], parts[1])
            own = v_ref[x, :, pl.ds(at, pair)].astype(jnp.float32)
            out_ref[x, :, pl.ds(at, pair)] = (1.5 * own - 0.5 * both).astype(jnp.bfloat16)
        return carry

    lax.fori_loop(0, slot_count // 2, compact, 0)


def kernel(lines_per_layer, device_count, row_count, mask_ref, dense, total, res_ref,
           square, zbuf, ybuf, gbuf, zsend, zrecv, ysend, yrecv, gsend, grecv):
    span = dense.shape[2]
    block = span // row_count
    pair = 2 * block
    halves = row_count // 2

    me = lax.axis_index("grid")
    y = lax.rem(me, lines_per_layer)
    layer = me - y
    y_up = layer + lax.rem(y + 1, lines_per_layer)
    y_down = layer + lax.rem(y + lines_per_layer - 1, lines_per_layer)
    z_up = lax.rem(me + lines_per_layer, device_count)
    z_down = lax.rem(me + device_count - lines_per_layer, device_count)
    y_to = (y_up, y_down)
    z_to = (z_up, z_down)

    barrier = pltpu.get_barrier_semaphore()
    for other in (z_up, z_down, y_up, y_down):
        pl.semaphore_signal(barrier, inc=1, device_id={"grid": other}, device_id_type=MESH)

    pl.semaphore_wait(barrier, 4)

    def remote(src, dst, send, recv, to):
        return pltpu.make_async_remote_copy(
            src_ref=src, dst_ref=dst, send_sem=send, recv_sem=recv,
            device_id={"grid": to}, device_id_type=MESH,
        )

    def product(phase, right):
        def z_copy(d, k):
            return remote(right.at[1 - d + k], zbuf.at[phase, d, k],
                          zsend.at[phase, d, k], zrecv.at[phase, d, k], z_to[d])

        def y_copy(d):
            return remote(right.at[:, pl.ds(1 - d, 2)], ybuf.at[phase, d],
                          ysend.at[phase, d], yrecv.at[phase, d], y_to[d])

        def g_copy(zd, yd, k):
            return remote(zbuf.at[phase, zd, k, pl.ds(1 - yd, 2)], gbuf.at[phase, zd, yd, k],
                          gsend.at[phase, zd, yd, k], grecv.at[phase, zd, yd, k], y_to[yd])

        def accumulate(mz, my, source, nz, ny, z0, y0, first=False):
            def step(i, carry):
                kz, ky = i // ny, i % ny
                part = jnp.dot(dense[mz, my], source(kz, ky), preferred_element_type=jnp.float32)
                c = (z0 + kz) * 3 + y0 + ky
                for h in range(halves):
                    piece = part[:, h * pair:(h + 1) * pair]
                    if first:
                        total[c * halves + h] = piece
                    else:
                        total[c * halves + h] += piece
                return carry

            lax.fori_loop(0, nz * ny, step, 0)

        for k in range(2):
            for d in range(2):
                z_copy(d, k).start()
        for d in range(2):
            y_copy(d).start()
        accumulate(1, 1, lambda kz, ky: right[kz, ky], 3, 3, 0, 0, first=True)
        for k in range(2):
            for zd in range(2):
                z_copy(zd, k).wait_recv()
                for yd in range(2):
                    g_copy(zd, yd, k).start()
        for d in range(2):
            accumulate(2 * d, 1, lambda kz, ky: zbuf[phase, d, kz, ky], 2, 3, d, 0)
        for d in range(2):
            y_copy(d).wait_recv()
            accumulate(1, 2 * d, lambda kz, ky: ybuf[phase, d, kz, ky], 3, 2, 0, d)
        for zd in range(2):
            for yd in range(2):
                for k in range(2):
                    g_copy(zd, yd, k).wait_recv()
                accumulate(2 * zd, 2 * yd, lambda kz, ky: gbuf[phase, zd, yd, kz, ky], 2, 2, zd, yd)

        def finish():
            for d in range(2):
                y_copy(d).wait_send()
                for k in range(2):
                    z_copy(d, k).wait_send()
                    for yd in range(2):
                        g_copy(d, yd, k).wait_send()

        return finish

    finish_values = product(0, dense)

    sublane = lax.broadcasted_iota(jnp.int32, (block, pair), 0)
    lane = lax.broadcasted_iota(jnp.int32, (block, pair), 1)

    def to_square(c, carry):
        for x in range(row_count):
            rows = pl.ds(x * block, block)
            for h in range(halves):
                kept = mask_ref[c, pl.ds(x, 1), pl.ds(h * pair, pair)] > 0.0
                tile = jnp.where(kept, total[c * halves + h, rows, :], 0.0).astype(jnp.bfloat16)
                square[c // 3, c % 3, rows, pl.ds(h * pair, pair)] = tile
                deviation = tile.astype(jnp.float32)
                if x // 2 == h:
                    on_diagonal = lane == sublane + (x % 2) * block
                    weight = jnp.where(c == 4, 1.0, 0.0)
                    deviation = deviation - jnp.where(on_diagonal, weight, 0.0)
                squares = deviation * deviation
                carry = carry + jnp.sum(squares.reshape(block // 8, 8, pair), axis=0)
        return carry

    res_ref[...] = lax.fori_loop(0, 9, to_square, jnp.zeros((8, pair), jnp.float32))

    finish_square = product(1, square)

    finish_values()
    finish_square()


def on_device(values, pattern):
    row_count, block_size, panel_width = values.shape
    device_count = lax.axis_size("grid")
    lines_per_layer = device_count // LAYERS
    total_rows = row_count * device_count
    line_index = lax.axis_index("grid")
    place, slot_at, mask = tile_tables(pattern, line_index, lines_per_layer, row_count, block_size)
    span = row_count * block_size
    pair = 2 * block_size
    vmem = pl.BlockSpec(memory_space=pltpu.VMEM)
    smem = pl.BlockSpec(memory_space=pltpu.SMEM)
    dma = pltpu.SemaphoreType.DMA
    dense = pl.pallas_call(
        expand_kernel,
        out_shape=jax.ShapeDtypeStruct((3, 3, span, span), jnp.bfloat16),
        in_specs=[smem, vmem],
        out_specs=vmem,
    )(slot_at, values)
    total, squares = pl.pallas_call(
        functools.partial(kernel, lines_per_layer, device_count, row_count),
        out_shape=(
            jax.ShapeDtypeStruct((9 * row_count // 2, span, pair), jnp.float32),
            jax.ShapeDtypeStruct((8, pair), jnp.float32),
        ),
        in_specs=[vmem, vmem],
        out_specs=(vmem, vmem),
        scratch_shapes=[
            pltpu.VMEM((3, 3, span, span), jnp.bfloat16),
            pltpu.VMEM((2, 2, 2, 3, span, span), jnp.bfloat16),
            pltpu.VMEM((2, 2, 3, 2, span, span), jnp.bfloat16),
            pltpu.VMEM((2, 2, 2, 2, 2, span, span), jnp.bfloat16),
            dma((2, 2, 2)),
            dma((2, 2, 2)),
            dma((2, 2)),
            dma((2, 2)),
            dma((2, 2, 2, 2)),
            dma((2, 2, 2, 2)),
        ],
        compiler_params=pltpu.CompilerParams(
            collective_id=0, has_side_effects=True, vmem_limit_bytes=40 * 1024 * 1024
        ),
    )(mask, dense)
    updated = pl.pallas_call(
        compact_kernel,
        out_shape=jax.ShapeDtypeStruct(values.shape, jnp.bfloat16),
        in_specs=[smem, vmem, vmem],
        out_specs=vmem,
    )(place, total, values)
    residual = lax.psum(jnp.sum(squares), "grid") / (total_rows * block_size)
    return (updated, residual.reshape(1))


def solution(mesh):
    in_specs = (P(("groups", "grid"), None, None), P())
    out_specs = (P(("groups", "grid"), None, None), P("groups"))
    return jax.shard_map(
        on_device, mesh=mesh, in_specs=in_specs, out_specs=out_specs, check_vma=False
    )
```

time: 470 us -> 143 us (0.30)
  local copies, waits for them, and re-layouts: 182 us -> 4.29 us
  waiting for transfers between devices: 105 us -> 0 us
  Pallas kernels: 0 us -> 99.5 us
  blocking collectives: 101 us -> 34.7 us
  other arithmetic: 38.1 us -> 1.54 us
  matrix products: 19.3 us -> 0 us
  starting transfers between devices: 19.2 us -> 0 us
    gather x9 -> x0, local copies, waits for them, and re-layouts: 106 us -> none  [the longest x4 105 us: row_product(): selected = tile_view[local_rows[None, :], :, chosen_slot, :]]
    ppermute x12 -> x0, waiting for transfers between devices: 105 us -> none  [passed_along(): return lax.ppermute(block, axis, route)]
    pallas_call x0 -> x3, Pallas kernels: none -> 99.5 us  [the longest x1 92 us: on_device(): pl.pallas_call(functools.partial(kernel, lines_per_layer, device_count, r...]
    psum x1, blocking collectives: 101 us -> 34.7 us  [on_device(): residual = lax.psum(jnp.sum(squares), 'grid') / (total_rows * block_size)]
    reshape x4 -> x2, local copies, waits for them, and re-layouts: 55.6 us -> 0.7 us  [the longest x1 0.59 us: tile_tables(): return (place.reshape(-1), slot_at.reshape(-1), mask.transpose(1, 0, 2))]
    select_n x7 -> x0, other arithmetic: 21.7 us -> none  [the longest x2 21.4 us: row_product(): jnp.where(present[:, :, None, None], selected, jnp.zeros((), window.dtype))]
    dot_general x2 -> x0, matrix products: 19.3 us -> none  [row_product(): jnp.einsum('ax,kxc->akc', row_panel, stacked, preferred_element_type=jnp....]
    ppermute x12 -> x0, starting transfers between devices: 19.2 us -> none  [passed_along(): return lax.ppermute(block, axis, route)]
  transfers between devices with their start and end apart: 12 -> 0, of which waited for: 7 -> 0; matrix products, arithmetic and copies ran while one was open for 5% -> 0% of each run, Pallas kernels for 0% -> 0%
where the time goes in v1:
time: 143 us
  Pallas kernels  99.5 us (70%)
  blocking collectives  34.7 us (24%)
  local copies, waits for them, and re-layouts  4.29 us (3%)
  between operations  2.49 us (2%)
  other arithmetic  1.54 us (1%)
    pallas_call x1, Pallas kernels, on_device(): pl.pallas_call(functools.partial(kernel, lines_per_layer, device_count, r...  92 us
    psum x1, blocking collectives, on_device(): residual = lax.psum(jnp.sum(squares), 'grid') / (total_rows * block_size)  34.7 us
    pallas_call x1, Pallas kernels, on_device(): pl.pallas_call(compact_kernel, out_shape=jax.ShapeDtypeStruct(values.shap...  3.87 us
    pallas_call x1, Pallas kernels, on_device(): pl.pallas_call(expand_kernel, out_shape=jax.ShapeDtypeStruct((3, 3, span,...  3.63 us

profile of v1, /device:TPU:0, one launch (start us, length us, event | category | flops | bytes accessed | tf_op | source)
XLA Modules:
  0.0 142.5 jit_solution(3293242544168381835)
XLA Ops:
  0.7 0.8 fusion.7
  1.5 0.1 select_reduce_fusion
  1.6 0.1 copy.9
  1.7 0.6 reshape.26.place_ref
  2.3 0.6 sub.45.slot_ref
  2.9 0.1 reshape.29
  3.0 0.1 broadcast_in_dim.15
  3.1 0.1 reshape.27
  3.2 3.6 %shard_map.41.dense = bf16[3,3,256,256]{3,2,1,0:T(8,128)(2,1)} custom-call(s32[144]{0:T(256)} %sub.45.slot_ref, bf16[4,64,1152]{2,1,0:T(8,128)(2,1)} %v_ref.3), custom_call_target="tpu_custom_call" | custom-call | tf_op jit(solution)/shard_map/pallas_call | solution.py:219
  6.9 0.0 copy-start
  6.9 1.3 copy-done
  8.1 92.0 %shard_map.42 = (f32[18,256,128]{2,1,0:T(8,128)S(1)}, f32[8,128]{1,0:T(8,128)S(1)}) custom-call(f32[9,4,256]{2,1,0:T(4,128)S(1)} %bitcast.4, bf16[3,3,256,256]{3,2,1,0:T(8,128)(2,1)S(1)} %copy-done), custom_call_target="tpu_custom_call" | custom-call | tf_op jit(solution)/shard_map/pallas_call | solution.py:225
  100.2 0.0 copy-start.1
  100.2 1.4 copy-done.1
  101.6 0.6 reduce_sum.19
  102.2 34.7 %psum.7 = f32[]{:T(128)} all-reduce(f32[]{:T(128)} %reduce_sum.19), channel_id=1, replica_groups=mesh['groups'=2,'grid'=16] {'grid'}, use_global_device_ids=true, to_apply=%region_2.3 | all-reduce | flops 1 | bytes 8 | tf_op jit(solution)/shard_map/psum | solution.py:255
  137.5 3.9 %shard_map.43 = bf16[4,64,1152]{2,1,0:T(8,128)(2,1)} custom-call(s32[72]{0:T(128)} %reshape.26.place_ref, f32[18,256,128]{2,1,0:T(8,128)} %copy-done.1, bf16[4,64,1152]{2,1,0:T(8,128)(2,1)} %v_ref.3), custom_call_target="tpu_custom_call" | custom-call | tf_op jit(solution)/shard_map/pallas_call | solution.py:249
  (4 shorter events, 0.0 us)
Async XLA Ops:
  6.9 1.3 copy-start
  100.2 1.4 copy-start.1

commit v2 on v1

--- a/solution.py
+++ b/solution.py
@@ -87,7 +87,7 @@
 
 
 def kernel(lines_per_layer, device_count, row_count, mask_ref, dense, total, res_ref,
-           square, zbuf, ybuf, gbuf, zsend, zrecv, ysend, yrecv, gsend, grecv):
+           square, zbuf, ybuf, gbuf, zsend, zrecv, ysend, yrecv, gsend, grecv, ring, ring_send, ring_recv):
     span = dense.shape[2]
     block = span // row_count
     pair = 2 * block
@@ -115,7 +115,37 @@
             device_id={"grid": to}, device_id_type=MESH,
         )
 
-    def product(phase, right):
+    hops = [y_up] * (lines_per_layer - 1) + [z_up] * (LAYERS - 1)
+    turn = lines_per_layer - 1
+
+    def ring_copy(hop):
+        return remote(ring.at[hop + (hop >= turn)], ring.at[hop + 1 + (hop >= turn)],
+                      ring_send.at[hop], ring_recv.at[hop], hops[hop])
+
+    def ring_sum(start, place, length):
+        summed = ring[start + place]
+        for other in range(1, length):
+            summed = summed + ring[start + lax.rem(place + length - other, length)]
+        return summed
+
+    def ring_hop(hop):
+        ring_copy(hop).wait_recv()
+        if hop + 1 == turn:
+            ring[turn + 1] = ring_sum(0, y, lines_per_layer)
+        if hop + 1 < len(hops):
+            ring_copy(hop + 1).start()
+        else:
+            res_ref[...] = ring_sum(turn + 1, layer // lines_per_layer, LAYERS)
+
+    def product(phase, right, hop_list=()):
+        waiting = list(hop_list)
+        share = -(-len(waiting) // 6)
+
+        def between():
+            for hop in waiting[:share]:
+                ring_hop(hop)
+            del waiting[:share]
+
         def z_copy(d, k):
             return remote(right.at[1 - d + k], zbuf.at[phase, d, k],
                           zsend.at[phase, d, k], zrecv.at[phase, d, k], z_to[d])
@@ -149,16 +179,20 @@
         for d in range(2):
             y_copy(d).start()
         accumulate(1, 1, lambda kz, ky: right[kz, ky], 3, 3, 0, 0, first=True)
+        between()
         for k in range(2):
             for zd in range(2):
                 z_copy(zd, k).wait_recv()
                 for yd in range(2):
                     g_copy(zd, yd, k).start()
+            between()
         for d in range(2):
             accumulate(2 * d, 1, lambda kz, ky: zbuf[phase, d, kz, ky], 2, 3, d, 0)
+            between()
         for d in range(2):
             y_copy(d).wait_recv()
             accumulate(1, 2 * d, lambda kz, ky: ybuf[phase, d, kz, ky], 3, 2, 0, d)
+            between()
         for zd in range(2):
             for yd in range(2):
                 for k in range(2):
@@ -196,12 +230,16 @@
                 carry = carry + jnp.sum(squares.reshape(block // 8, 8, pair), axis=0)
         return carry
 
-    res_ref[...] = lax.fori_loop(0, 9, to_square, jnp.zeros((8, pair), jnp.float32))
-
-    finish_square = product(1, square)
+    squares = lax.fori_loop(0, 9, to_square, jnp.zeros((8, pair), jnp.float32))
+    ring[0] = squares
+    ring_copy(0).start()
+
+    finish_square = product(1, square, range(len(hops)))
 
     finish_values()
     finish_square()
+    for hop in range(len(hops)):
+        ring_copy(hop).wait_send()
 
 
 def on_device(values, pattern):
@@ -241,6 +279,9 @@
             dma((2, 2)),
             dma((2, 2, 2, 2)),
             dma((2, 2, 2, 2)),
+            pltpu.VMEM((lines_per_layer + LAYERS, 8, pair), jnp.float32),
+            dma((lines_per_layer + LAYERS - 2,)),
+            dma((lines_per_layer + LAYERS - 2,)),
         ],
         compiler_params=pltpu.CompilerParams(
             collective_id=0, has_side_effects=True, vmem_limit_bytes=40 * 1024 * 1024
@@ -252,7 +293,7 @@
         in_specs=[smem, vmem, vmem],
         out_specs=vmem,
     )(place, total, values)
-    residual = lax.psum(jnp.sum(squares), "grid") / (total_rows * block_size)
+    residual = jnp.sum(squares) / (total_rows * block_size)
     return (updated, residual.reshape(1))
 
 

time: 143 us -> 114 us (0.80)
  blocking collectives: 34.7 us -> 0 us
  Pallas kernels: 99.5 us -> 106 us
    psum x1 -> x0, blocking collectives: 34.7 us -> none  [on_device(): residual = lax.psum(jnp.sum(squares), 'grid') / (total_rows * block_size)]
    pallas_call x1, Pallas kernels: 92 us -> 98.4 us  [on_device(): pl.pallas_call(functools.partial(kernel, lines_per_layer, device_count, r...]
where the time goes in v2:
time: 114 us
  Pallas kernels  106 us (93%)
  local copies, waits for them, and re-layouts  4.29 us (4%)
  between operations  2.49 us (2%)
  other arithmetic  1.54 us (1%)
    pallas_call x1, Pallas kernels, on_device(): pl.pallas_call(functools.partial(kernel, lines_per_layer, device_count, r...  98.4 us
    pallas_call x1, Pallas kernels, on_device(): pl.pallas_call(compact_kernel, out_shape=jax.ShapeDtypeStruct(values.shap...  3.87 us
    pallas_call x1, Pallas kernels, on_device(): pl.pallas_call(expand_kernel, out_shape=jax.ShapeDtypeStruct((3, 3, span,...  3.63 us
    unnamed x4, local copies, waits for them, and re-layouts  2.68 us

profile of v2, /device:TPU:0, one launch (start us, length us, event | category | flops | bytes accessed | tf_op | source)
XLA Modules:
  0.0 114.2 jit_solution(16454836113509620139)
XLA Ops:
  0.7 0.8 fusion.7
  1.5 0.1 select_reduce_fusion
  1.6 0.1 copy.9
  1.7 0.6 reshape.26.place_ref
  2.3 0.6 sub.45.slot_ref
  2.9 0.1 reshape.29
  3.0 0.1 broadcast_in_dim.15
  3.1 0.1 reshape.27
  3.2 3.6 %shard_map.41.dense = bf16[3,3,256,256]{3,2,1,0:T(8,128)(2,1)} custom-call(s32[144]{0:T(256)} %sub.45.slot_ref, bf16[4,64,1152]{2,1,0:T(8,128)(2,1)} %v_ref.3), custom_call_target="tpu_custom_call" | custom-call | tf_op jit(solution)/shard_map/pallas_call | solution.py:257
  6.9 0.0 copy-start
  6.9 1.3 %copy-done = bf16[3,3,256,256]{3,2,1,0:T(8,128)(2,1)S(1)} copy-done((bf16[3,3,256,256]{3,2,1,0:T(8,128)(2,1)S(1)}, bf16[3,3,256,256]{3,2,1,0:T(8,128)(2,1)}, u32[]{:S(2)}) %copy-start) | copy-done | bytes 1179672
  8.1 98.4 %shard_map.42 = (f32[18,256,128]{2,1,0:T(8,128)S(1)}, f32[8,128]{1,0:T(8,128)S(1)}) custom-call(f32[9,4,256]{2,1,0:T(4,128)S(1)} %bitcast.4, bf16[3,3,256,256]{3,2,1,0:T(8,128)(2,1)S(1)} %copy-done), custom_call_target="tpu_custom_call" | custom-call | tf_op jit(solution)/shard_map/pallas_call | solution.py:263
  106.5 0.0 copy-start.1
  106.5 1.4 %copy-done.1 = f32[18,256,128]{2,1,0:T(8,128)} copy-done((f32[18,256,128]{2,1,0:T(8,128)}, f32[18,256,128]{2,1,0:T(8,128)S(1)}, u32[]{:S(2)}) %copy-start.1) | copy-done | bytes 2359320
  107.9 0.6 reduce_sum.19
  109.2 3.9 %shard_map.43 = bf16[4,64,1152]{2,1,0:T(8,128)(2,1)} custom-call(s32[72]{0:T(128)} %reshape.26.place_ref, f32[18,256,128]{2,1,0:T(8,128)} %copy-done.1, bf16[4,64,1152]{2,1,0:T(8,128)(2,1)} %v_ref.3), custom_call_target="tpu_custom_call" | custom-call | tf_op jit(solution)/shard_map/pallas_call | solution.py:290
  (4 shorter events, 0.0 us)
Async XLA Ops:
  6.9 1.3 %copy-start = (bf16[3,3,256,256]{3,2,1,0:T(8,128)(2,1)S(1)}, bf16[3,3,256,256]{3,2,1,0:T(8,128)(2,1)}, u32[]{:S(2)}) copy-start(bf16[3,3,256,256]{3,2,1,0:T(8,128)(2,1)} %shard_map.41.dense) | copy-start | bytes 3538948
  106.5 1.4 %copy-start.1 = (f32[18,256,128]{2,1,0:T(8,128)}, f32[18,256,128]{2,1,0:T(8,128)S(1)}, u32[]{:S(2)}) copy-start(f32[18,256,128]{2,1,0:T(8,128)S(1)} %get-tuple-element.4.total) | copy-start | bytes 7077892

commit v3 on v1

--- a/solution.py
+++ b/solution.py
@@ -86,28 +86,56 @@
     lax.fori_loop(0, slot_count // 2, compact, 0)
 
 
-def kernel(lines_per_layer, device_count, row_count, mask_ref, dense, total, res_ref,
-           square, zbuf, ybuf, gbuf, zsend, zrecv, ysend, yrecv, gsend, grecv):
+def kernel(lines_per_layer, device_count, mask_ref, dense, total, res_ref,
+           packed, zbuf, ybuf, gbuf, zsend, zrecv, ysend, yrecv, gsend, grecv,
+           bank, bank_send, bank_recv):
     span = dense.shape[2]
-    block = span // row_count
+    block = span // 4
     pair = 2 * block
-    halves = row_count // 2
 
     me = lax.axis_index("grid")
     y = lax.rem(me, lines_per_layer)
     layer = me - y
-    y_up = layer + lax.rem(y + 1, lines_per_layer)
-    y_down = layer + lax.rem(y + lines_per_layer - 1, lines_per_layer)
-    z_up = lax.rem(me + lines_per_layer, device_count)
-    z_down = lax.rem(me + device_count - lines_per_layer, device_count)
-    y_to = (y_up, y_down)
-    z_to = (z_up, z_down)
+    y_peers = [layer + lax.rem(y + o, lines_per_layer) for o in range(1, lines_per_layer)]
+    z_peers = [lax.rem(me + o * lines_per_layer, device_count) for o in range(1, LAYERS)]
+    y_to = (y_peers[0], y_peers[-1])
+    z_to = (z_peers[0], z_peers[-1])
 
     barrier = pltpu.get_barrier_semaphore()
-    for other in (z_up, z_down, y_up, y_down):
+    for other in y_peers + z_peers:
         pl.semaphore_signal(barrier, inc=1, device_id={"grid": other}, device_id_type=MESH)
 
-    pl.semaphore_wait(barrier, 4)
+    def rows_of(x):
+        return pl.ds(x * block, block)
+
+    def half_of(h):
+        return pl.ds(h * pair, pair)
+
+    def pack(c, carry):
+        cz, cy = c // 3, c % 3
+        for x in range(4):
+            packed[0, cz, cy, rows_of(x), :] = dense[cz, cy, rows_of(x), half_of(x // 2)]
+        for h in range(2):
+            first, second = 2 * (1 - h), 2 * (1 - h) + 1
+            packed[0, cz, cy, rows_of(4 + h), :] = (
+                dense[cz, cy, rows_of(first), half_of(h)] + dense[cz, cy, rows_of(second), half_of(h)]
+            )
+        return carry
+
+    lax.fori_loop(0, 9, pack, 0)
+    pl.semaphore_wait(barrier, len(y_peers) + len(z_peers))
+
+    low = low_half(block)
+    zero = jnp.zeros((block, pair), jnp.bfloat16)
+
+    def unpacked(ref):
+        mixed = [ref[rows_of(4 + h), :] for h in range(2)]
+        whole = ref[pl.ds(0, span), :]
+        left = [whole[: 2 * block], jnp.where(low, zero, mixed[0]), jnp.where(low, mixed[0], zero)]
+        right = [jnp.where(low, zero, mixed[1]), jnp.where(low, mixed[1], zero), whole[2 * block:]]
+        return jnp.concatenate(
+            [jnp.concatenate(left, axis=0), jnp.concatenate(right, axis=0)], axis=1
+        )
 
     def remote(src, dst, send, recv, to):
         return pltpu.make_async_remote_copy(
@@ -115,7 +143,30 @@
             device_id={"grid": to}, device_id_type=MESH,
         )
 
-    def product(phase, right):
+    def bank_y(o):
+        return remote(bank.at[0], bank.at[o], bank_send.at[o - 1], bank_recv.at[o - 1], y_peers[o - 1])
+
+    def bank_z(o):
+        sem = lines_per_layer - 2 + o
+        return remote(bank.at[lines_per_layer], bank.at[lines_per_layer + o],
+                      bank_send.at[sem], bank_recv.at[sem], z_peers[o - 1])
+
+    def bank_sum(start, place, length):
+        summed = bank[start + place]
+        for other in range(1, length):
+            summed = summed + bank[start + lax.rem(place + length - other, length)]
+        return summed
+
+    def layer_sum():
+        for o in range(1, lines_per_layer):
+            bank_y(o).wait_recv()
+        bank[lines_per_layer] = bank_sum(0, y, lines_per_layer)
+        for o in range(1, LAYERS):
+            bank_z(o).start()
+
+    def product(phase, after_own):
+        right = packed.at[phase]
+
         def z_copy(d, k):
             return remote(right.at[1 - d + k], zbuf.at[phase, d, k],
                           zsend.at[phase, d, k], zrecv.at[phase, d, k], z_to[d])
@@ -131,14 +182,16 @@
         def accumulate(mz, my, source, nz, ny, z0, y0, first=False):
             def step(i, carry):
                 kz, ky = i // ny, i % ny
-                part = jnp.dot(dense[mz, my], source(kz, ky), preferred_element_type=jnp.float32)
+                part = jnp.dot(
+                    dense[mz, my], unpacked(source(kz, ky)), preferred_element_type=jnp.float32
+                )
                 c = (z0 + kz) * 3 + y0 + ky
-                for h in range(halves):
+                for h in range(2):
                     piece = part[:, h * pair:(h + 1) * pair]
                     if first:
-                        total[c * halves + h] = piece
+                        total[c * 2 + h] = piece
                     else:
-                        total[c * halves + h] += piece
+                        total[c * 2 + h] += piece
                 return carry
 
             lax.fori_loop(0, nz * ny, step, 0)
@@ -148,22 +201,28 @@
                 z_copy(d, k).start()
         for d in range(2):
             y_copy(d).start()
-        accumulate(1, 1, lambda kz, ky: right[kz, ky], 3, 3, 0, 0, first=True)
-        for k in range(2):
+
+        def relay(k):
             for zd in range(2):
                 z_copy(zd, k).wait_recv()
                 for yd in range(2):
                     g_copy(zd, yd, k).start()
-        for d in range(2):
-            accumulate(2 * d, 1, lambda kz, ky: zbuf[phase, d, kz, ky], 2, 3, d, 0)
+
+        accumulate(1, 1, lambda kz, ky: right.at[kz, ky], 3, 3, 0, 0, first=True)
+        after_own()
+        relay(0)
         for d in range(2):
             y_copy(d).wait_recv()
-            accumulate(1, 2 * d, lambda kz, ky: ybuf[phase, d, kz, ky], 3, 2, 0, d)
-        for zd in range(2):
-            for yd in range(2):
-                for k in range(2):
+            accumulate(1, 2 * d, lambda kz, ky: ybuf.at[phase, d, kz, ky], 3, 2, 0, d)
+        relay(1)
+        for d in range(2):
+            accumulate(2 * d, 1, lambda kz, ky: zbuf.at[phase, d, kz, ky], 2, 3, d, 0)
+        for k in range(2):
+            for zd in range(2):
+                for yd in range(2):
                     g_copy(zd, yd, k).wait_recv()
-                accumulate(2 * zd, 2 * yd, lambda kz, ky: gbuf[phase, zd, yd, kz, ky], 2, 2, zd, yd)
+                    accumulate(2 * zd, 2 * yd, lambda kz, ky: gbuf.at[phase, zd, yd, k, ky],
+                               1, 2, zd + k, yd)
 
         def finish():
             for d in range(2):
@@ -175,33 +234,50 @@
 
         return finish
 
-    finish_values = product(0, dense)
+    finish_values = product(0, lambda: None)
 
     sublane = lax.broadcasted_iota(jnp.int32, (block, pair), 0)
     lane = lax.broadcasted_iota(jnp.int32, (block, pair), 1)
 
     def to_square(c, carry):
-        for x in range(row_count):
-            rows = pl.ds(x * block, block)
-            for h in range(halves):
-                kept = mask_ref[c, pl.ds(x, 1), pl.ds(h * pair, pair)] > 0.0
-                tile = jnp.where(kept, total[c * halves + h, rows, :], 0.0).astype(jnp.bfloat16)
-                square[c // 3, c % 3, rows, pl.ds(h * pair, pair)] = tile
-                deviation = tile.astype(jnp.float32)
-                if x // 2 == h:
-                    on_diagonal = lane == sublane + (x % 2) * block
-                    weight = jnp.where(c == 4, 1.0, 0.0)
-                    deviation = deviation - jnp.where(on_diagonal, weight, 0.0)
-                squares = deviation * deviation
-                carry = carry + jnp.sum(squares.reshape(block // 8, 8, pair), axis=0)
+        cz, cy = c // 3, c % 3
+        weight = jnp.where(c == 4, 1.0, 0.0)
+
+        def kept(x, h):
+            mask = mask_ref[c, pl.ds(x, 1), half_of(h)] > 0.0
+            return jnp.where(mask, total[c * 2 + h, rows_of(x), :], 0.0)
+
+        for piece in range(6):
+            if piece < 4:
+                tile = kept(piece, piece // 2)
+            else:
+                h = piece - 4
+                tile = kept(2 * (1 - h), h) + kept(2 * (1 - h) + 1, h)
+            tile = tile.astype(jnp.bfloat16)
+            packed[1, cz, cy, rows_of(piece), :] = tile
+            deviation = tile.astype(jnp.float32)
+            if piece < 4:
+                on_diagonal = lane == sublane + (piece % 2) * block
+                deviation = deviation - jnp.where(on_diagonal, weight, 0.0)
+            squares = deviation * deviation
+            carry = carry + jnp.sum(squares.reshape(block // 8, 8, pair), axis=0)
         return carry
 
-    res_ref[...] = lax.fori_loop(0, 9, to_square, jnp.zeros((8, pair), jnp.float32))
-
-    finish_square = product(1, square)
-
+    bank[0] = lax.fori_loop(0, 9, to_square, jnp.zeros((8, pair), jnp.float32))
+    for o in range(1, lines_per_layer):
+        bank_y(o).start()
+
+    finish_square = product(1, layer_sum)
+
+    for o in range(1, LAYERS):
+        bank_z(o).wait_recv()
+    res_ref[...] = bank_sum(lines_per_layer, layer // lines_per_layer, LAYERS)
     finish_values()
     finish_square()
+    for o in range(1, lines_per_layer):
+        bank_y(o).wait_send()
+    for o in range(1, LAYERS):
+        bank_z(o).wait_send()
 
 
 def on_device(values, pattern):
@@ -213,6 +289,7 @@
     place, slot_at, mask = tile_tables(pattern, line_index, lines_per_layer, row_count, block_size)
     span = row_count * block_size
     pair = 2 * block_size
+    pieces = 6 * block_size
     vmem = pl.BlockSpec(memory_space=pltpu.VMEM)
     smem = pl.BlockSpec(memory_space=pltpu.SMEM)
     dma = pltpu.SemaphoreType.DMA
@@ -223,7 +300,7 @@
         out_specs=vmem,
     )(slot_at, values)
     total, squares = pl.pallas_call(
-        functools.partial(kernel, lines_per_layer, device_count, row_count),
+        functools.partial(kernel, lines_per_layer, device_count),
         out_shape=(
             jax.ShapeDtypeStruct((9 * row_count // 2, span, pair), jnp.float32),
             jax.ShapeDtypeStruct((8, pair), jnp.float32),
@@ -231,16 +308,19 @@
         in_specs=[vmem, vmem],
         out_specs=(vmem, vmem),
         scratch_shapes=[
-            pltpu.VMEM((3, 3, span, span), jnp.bfloat16),
-            pltpu.VMEM((2, 2, 2, 3, span, span), jnp.bfloat16),
-            pltpu.VMEM((2, 2, 3, 2, span, span), jnp.bfloat16),
-            pltpu.VMEM((2, 2, 2, 2, 2, span, span), jnp.bfloat16),
+            pltpu.VMEM((2, 3, 3, pieces, pair), jnp.bfloat16),
+            pltpu.VMEM((2, 2, 2, 3, pieces, pair), jnp.bfloat16),
+            pltpu.VMEM((2, 2, 3, 2, pieces, pair), jnp.bfloat16),
+            pltpu.VMEM((2, 2, 2, 2, 2, pieces, pair), jnp.bfloat16),
             dma((2, 2, 2)),
             dma((2, 2, 2)),
             dma((2, 2)),
             dma((2, 2)),
             dma((2, 2, 2, 2)),
             dma((2, 2, 2, 2)),
+            pltpu.VMEM((lines_per_layer + LAYERS, 8, pair), jnp.float32),
+            dma((lines_per_layer + LAYERS - 2,)),
+            dma((lines_per_layer + LAYERS - 2,)),
         ],
         compiler_params=pltpu.CompilerParams(
             collective_id=0, has_side_effects=True, vmem_limit_bytes=40 * 1024 * 1024
@@ -252,7 +332,7 @@
         in_specs=[smem, vmem, vmem],
         out_specs=vmem,
     )(place, total, values)
-    residual = lax.psum(jnp.sum(squares), "grid") / (total_rows * block_size)
+    residual = jnp.sum(squares) / (total_rows * block_size)
     return (updated, residual.reshape(1))
 
 

time: 143 us -> 87.4 us (0.61)
  blocking collectives: 34.7 us -> 0 us
  Pallas kernels: 99.5 us -> 78.8 us
    psum x1 -> x0, blocking collectives: 34.7 us -> none  [on_device(): residual = lax.psum(jnp.sum(squares), 'grid') / (total_rows * block_size)]
    pallas_call x1, Pallas kernels: 92 us -> 71.3 us  [on_device(): pl.pallas_call(functools.partial(kernel, lines_per_layer, device_count),...]
where the time goes in v3:
time: 87.4 us; the launch traced here: 87.1 us
  Pallas kernels  78.8 us (90%)
  local copies, waits for them, and re-layouts  4.29 us (5%)
  between operations  2.49 us (3%)
  other arithmetic  1.54 us (2%)
    pallas_call x1, Pallas kernels, on_device(): pl.pallas_call(functools.partial(kernel, lines_per_layer, device_count),...  71.3 us
    pallas_call x1, Pallas kernels, on_device(): pl.pallas_call(compact_kernel, out_shape=jax.ShapeDtypeStruct(values.shap...  3.87 us
    pallas_call x1, Pallas kernels, on_device(): pl.pallas_call(expand_kernel, out_shape=jax.ShapeDtypeStruct((3, 3, span,...  3.63 us
    unnamed x4, local copies, waits for them, and re-layouts  2.68 us

profile of v3, /device:TPU:0, one launch (start us, length us, event | category | flops | bytes accessed | tf_op | source)
XLA Modules:
  0.0 87.1 jit_solution(1517252201540087168)
XLA Ops:
  0.7 0.8 fusion.7
  1.5 0.1 select_reduce_fusion
  1.6 0.1 copy.9
  1.7 0.6 reshape.26.place_ref
  2.3 0.6 sub.45.slot_ref
  2.9 0.1 reshape.29
  3.0 0.1 broadcast_in_dim.15
  3.1 0.1 reshape.27
  3.2 3.6 %shard_map.41.dense = bf16[3,3,256,256]{3,2,1,0:T(8,128)(2,1)} custom-call(s32[144]{0:T(256)} %sub.45.slot_ref, bf16[4,64,1152]{2,1,0:T(8,128)(2,1)} %v_ref.3), custom_call_target="tpu_custom_call" | custom-call | tf_op jit(solution)/shard_map/pallas_call | solution.py:296
  6.9 0.0 copy-start
  6.9 1.3 %copy-done = bf16[3,3,256,256]{3,2,1,0:T(8,128)(2,1)S(1)} copy-done((bf16[3,3,256,256]{3,2,1,0:T(8,128)(2,1)S(1)}, bf16[3,3,256,256]{3,2,1,0:T(8,128)(2,1)}, u32[]{:S(2)}) %copy-start) | copy-done | bytes 1179672
  8.1 71.3 %shard_map.42 = (f32[18,256,128]{2,1,0:T(8,128)S(1)}, f32[8,128]{1,0:T(8,128)S(1)}) custom-call(f32[9,4,256]{2,1,0:T(4,128)S(1)} %bitcast.4, bf16[3,3,256,256]{3,2,1,0:T(8,128)(2,1)S(1)} %copy-done), custom_call_target="tpu_custom_call" | custom-call | tf_op jit(solution)/shard_map/pallas_call | solution.py:302
  79.5 0.0 copy-start.1
  79.5 1.4 %copy-done.1 = f32[18,256,128]{2,1,0:T(8,128)} copy-done((f32[18,256,128]{2,1,0:T(8,128)}, f32[18,256,128]{2,1,0:T(8,128)S(1)}, u32[]{:S(2)}) %copy-start.1) | copy-done | bytes 2359320
  80.9 0.6 reduce_sum.19
  82.1 3.9 %shard_map.43 = bf16[4,64,1152]{2,1,0:T(8,128)(2,1)} custom-call(s32[72]{0:T(128)} %reshape.26.place_ref, f32[18,256,128]{2,1,0:T(8,128)} %copy-done.1, bf16[4,64,1152]{2,1,0:T(8,128)(2,1)} %v_ref.3), custom_call_target="tpu_custom_call" | custom-call | tf_op jit(solution)/shard_map/pallas_call | solution.py:329
  (4 shorter events, 0.0 us)
Async XLA Ops:
  6.9 1.3 %copy-start = (bf16[3,3,256,256]{3,2,1,0:T(8,128)(2,1)S(1)}, bf16[3,3,256,256]{3,2,1,0:T(8,128)(2,1)}, u32[]{:S(2)}) copy-start(bf16[3,3,256,256]{3,2,1,0:T(8,128)(2,1)} %shard_map.41.dense) | copy-start | bytes 3538948
  79.5 1.4 %copy-start.1 = (f32[18,256,128]{2,1,0:T(8,128)}, f32[18,256,128]{2,1,0:T(8,128)S(1)}, u32[]{:S(2)}) copy-start(f32[18,256,128]{2,1,0:T(8,128)S(1)} %get-tuple-element.4.total) | copy-start | bytes 7077892

commit v4 on v3

--- a/solution.py
+++ b/solution.py
@@ -164,116 +164,144 @@
         for o in range(1, LAYERS):
             bank_z(o).start()
 
-    def product(phase, after_own):
-        right = packed.at[phase]
-
-        def z_copy(d, k):
-            return remote(right.at[1 - d + k], zbuf.at[phase, d, k],
-                          zsend.at[phase, d, k], zrecv.at[phase, d, k], z_to[d])
-
-        def y_copy(d):
-            return remote(right.at[:, pl.ds(1 - d, 2)], ybuf.at[phase, d],
-                          ysend.at[phase, d], yrecv.at[phase, d], y_to[d])
-
-        def g_copy(zd, yd, k):
-            return remote(zbuf.at[phase, zd, k, pl.ds(1 - yd, 2)], gbuf.at[phase, zd, yd, k],
-                          gsend.at[phase, zd, yd, k], grecv.at[phase, zd, yd, k], y_to[yd])
-
-        def accumulate(mz, my, source, nz, ny, z0, y0, first=False):
-            def step(i, carry):
-                kz, ky = i // ny, i % ny
-                part = jnp.dot(
-                    dense[mz, my], unpacked(source(kz, ky)), preferred_element_type=jnp.float32
-                )
-                c = (z0 + kz) * 3 + y0 + ky
-                for h in range(2):
-                    piece = part[:, h * pair:(h + 1) * pair]
-                    if first:
-                        total[c * 2 + h] = piece
-                    else:
-                        total[c * 2 + h] += piece
-                return carry
-
-            lax.fori_loop(0, nz * ny, step, 0)
-
-        for k in range(2):
+    def z_copy(phase, d, j):
+        plane = 1 if j == 0 else 2 * (1 - d)
+        return remote(packed.at[phase, plane], zbuf.at[phase, d, j],
+                      zsend.at[phase, d, j], zrecv.at[phase, d, j], z_to[d])
+
+    def y_copy(phase, d, plane):
+        return remote(packed.at[phase, plane, pl.ds(1 - d, 2)], ybuf.at[phase, d, plane],
+                      ysend.at[phase, d, plane], yrecv.at[phase, d, plane], y_to[d])
+
+    def g_copy(phase, zd, yd, j):
+        return remote(zbuf.at[phase, zd, j, pl.ds(1 - yd, 2)], gbuf.at[phase, zd, yd, j],
+                      gsend.at[phase, zd, yd, j], grecv.at[phase, zd, yd, j], y_to[yd])
+
+    def place_of(d, j):
+        return 2 * d if j == 0 else 1
+
+    def send_z(phase, j):
+        for d in range(2):
+            z_copy(phase, d, j).start()
+
+    def send_y(phase, planes):
+        for plane in planes:
             for d in range(2):
-                z_copy(d, k).start()
+                y_copy(phase, d, plane).start()
+
+    def relay(phase, j):
+        for zd in range(2):
+            z_copy(phase, zd, j).wait_recv()
+            for yd in range(2):
+                g_copy(phase, zd, yd, j).start()
+
+    def accumulate(mz, my, source, nz, ny, z0, y0, first=False):
+        def step(i, carry):
+            kz, ky = i // ny, i % ny
+            part = jnp.dot(
+                dense[mz, my], unpacked(source(kz, ky)), preferred_element_type=jnp.float32
+            )
+            c = (z0 + kz) * 3 + y0 + ky
+            for h in range(2):
+                piece = part[:, h * pair:(h + 1) * pair]
+                if first:
+                    total[c * 2 + h] = piece
+                else:
+                    total[c * 2 + h] += piece
+            return carry
+
+        lax.fori_loop(0, nz * ny, step, 0)
+
+    def add_own(phase):
+        accumulate(1, 1, lambda kz, ky: packed.at[phase, kz, ky], 3, 3, 0, 0, first=True)
+
+    def add_y(phase):
         for d in range(2):
-            y_copy(d).start()
-
-        def relay(k):
-            for zd in range(2):
-                z_copy(zd, k).wait_recv()
-                for yd in range(2):
-                    g_copy(zd, yd, k).start()
-
-        accumulate(1, 1, lambda kz, ky: right.at[kz, ky], 3, 3, 0, 0, first=True)
-        after_own()
-        relay(0)
+            for plane in range(3):
+                y_copy(phase, d, plane).wait_recv()
+            accumulate(1, 2 * d, lambda kz, ky: ybuf.at[phase, d, kz, ky], 3, 2, 0, d)
+
+    def add_z(phase, j):
         for d in range(2):
-            y_copy(d).wait_recv()
-            accumulate(1, 2 * d, lambda kz, ky: ybuf.at[phase, d, kz, ky], 3, 2, 0, d)
-        relay(1)
-        for d in range(2):
-            accumulate(2 * d, 1, lambda kz, ky: zbuf.at[phase, d, kz, ky], 2, 3, d, 0)
-        for k in range(2):
-            for zd in range(2):
-                for yd in range(2):
-                    g_copy(zd, yd, k).wait_recv()
-                    accumulate(2 * zd, 2 * yd, lambda kz, ky: gbuf.at[phase, zd, yd, k, ky],
-                               1, 2, zd + k, yd)
-
-        def finish():
-            for d in range(2):
-                y_copy(d).wait_send()
-                for k in range(2):
-                    z_copy(d, k).wait_send()
-                    for yd in range(2):
-                        g_copy(d, yd, k).wait_send()
-
-        return finish
-
-    finish_values = product(0, lambda: None)
+            accumulate(2 * d, 1, lambda kz, ky: zbuf.at[phase, d, j, ky], 1, 3, place_of(d, j), 0)
+
+    def add_g(phase, j):
+        for zd in range(2):
+            for yd in range(2):
+                g_copy(phase, zd, yd, j).wait_recv()
+                accumulate(2 * zd, 2 * yd, lambda kz, ky: gbuf.at[phase, zd, yd, j, ky],
+                           1, 2, place_of(zd, j), yd)
 
     sublane = lax.broadcasted_iota(jnp.int32, (block, pair), 0)
     lane = lax.broadcasted_iota(jnp.int32, (block, pair), 1)
 
-    def to_square(c, carry):
-        cz, cy = c // 3, c % 3
-        weight = jnp.where(c == 4, 1.0, 0.0)
-
-        def kept(x, h):
-            mask = mask_ref[c, pl.ds(x, 1), half_of(h)] > 0.0
-            return jnp.where(mask, total[c * 2 + h, rows_of(x), :], 0.0)
-
-        for piece in range(6):
-            if piece < 4:
-                tile = kept(piece, piece // 2)
-            else:
-                h = piece - 4
-                tile = kept(2 * (1 - h), h) + kept(2 * (1 - h) + 1, h)
-            tile = tile.astype(jnp.bfloat16)
-            packed[1, cz, cy, rows_of(piece), :] = tile
-            deviation = tile.astype(jnp.float32)
-            if piece < 4:
-                on_diagonal = lane == sublane + (piece % 2) * block
-                deviation = deviation - jnp.where(on_diagonal, weight, 0.0)
-            squares = deviation * deviation
-            carry = carry + jnp.sum(squares.reshape(block // 8, 8, pair), axis=0)
-        return carry
-
-    bank[0] = lax.fori_loop(0, 9, to_square, jnp.zeros((8, pair), jnp.float32))
+    def to_square(cz):
+        def step(cy, carry):
+            c = cz * 3 + cy
+            weight = jnp.where(c == 4, 1.0, 0.0)
+
+            def kept(x, h):
+                mask = mask_ref[c, pl.ds(x, 1), half_of(h)] > 0.0
+                return jnp.where(mask, total[c * 2 + h, rows_of(x), :], 0.0)
+
+            for piece in range(6):
+                if piece < 4:
+                    tile = kept(piece, piece // 2)
+                else:
+                    h = piece - 4
+                    tile = kept(2 * (1 - h), h) + kept(2 * (1 - h) + 1, h)
+                tile = tile.astype(jnp.bfloat16)
+                packed[1, cz, cy, rows_of(piece), :] = tile
+                deviation = tile.astype(jnp.float32)
+                if piece < 4:
+                    on_diagonal = lane == sublane + (piece % 2) * block
+                    deviation = deviation - jnp.where(on_diagonal, weight, 0.0)
+                squares = deviation * deviation
+                carry = carry + jnp.sum(squares.reshape(block // 8, 8, pair), axis=0)
+            return carry
+
+        return lax.fori_loop(0, 3, step, jnp.zeros((8, pair), jnp.float32))
+
+    send_z(0, 0)
+    send_y(0, (0, 2, 1))
+    send_z(0, 1)
+    add_own(0)
+    relay(0, 0)
+    add_y(0)
+    add_z(0, 0)
+    add_g(0, 0)
+    outer = to_square(0) + to_square(2)
+    send_z(1, 1)
+    relay(0, 1)
+    send_y(1, (0, 2))
+    add_z(0, 1)
+    add_g(0, 1)
+    bank[0] = outer + to_square(1)
     for o in range(1, lines_per_layer):
         bank_y(o).start()
-
-    finish_square = product(1, layer_sum)
+    send_z(1, 0)
+    send_y(1, (1,))
+    relay(1, 1)
+    add_own(1)
+    layer_sum()
+    add_z(1, 1)
+    add_y(1)
+    relay(1, 0)
+    add_z(1, 0)
+    add_g(1, 1)
+    add_g(1, 0)
 
     for o in range(1, LAYERS):
         bank_z(o).wait_recv()
     res_ref[...] = bank_sum(lines_per_layer, layer // lines_per_layer, LAYERS)
-    finish_values()
-    finish_square()
+    for phase in range(2):
+        for d in range(2):
+            for plane in range(3):
+                y_copy(phase, d, plane).wait_send()
+            for j in range(2):
+                z_copy(phase, d, j).wait_send()
+                for yd in range(2):
+                    g_copy(phase, d, yd, j).wait_send()
     for o in range(1, lines_per_layer):
         bank_y(o).wait_send()
     for o in range(1, LAYERS):
@@ -314,8 +342,8 @@
             pltpu.VMEM((2, 2, 2, 2, 2, pieces, pair), jnp.bfloat16),
             dma((2, 2, 2)),
             dma((2, 2, 2)),
-            dma((2, 2)),
-            dma((2, 2)),
+            dma((2, 2, 3)),
+            dma((2, 2, 3)),
             dma((2, 2, 2, 2)),
             dma((2, 2, 2, 2)),
             pltpu.VMEM((lines_per_layer + LAYERS, 8, pair), jnp.float32),

time: 87.4 us -> 84.8 us (0.970)
  Pallas kernels: 78.8 us -> 75.9 us
    pallas_call x1, Pallas kernels: 71.3 us -> 68.4 us  [on_device(): pl.pallas_call(functools.partial(kernel, lines_per_layer, device_count),...]
where the time goes in v4:
time: 84.8 us; the launch traced here: 84.2 us
  Pallas kernels  75.9 us (90%)
  local copies, waits for them, and re-layouts  4.29 us (5%)
  between operations  2.49 us (3%)
  other arithmetic  1.54 us (2%)
    pallas_call x1, Pallas kernels, on_device(): pl.pallas_call(functools.partial(kernel, lines_per_layer, device_count),...  68.4 us
    pallas_call x1, Pallas kernels, on_device(): pl.pallas_call(compact_kernel, out_shape=jax.ShapeDtypeStruct(values.shap...  3.87 us
    pallas_call x1, Pallas kernels, on_device(): pl.pallas_call(expand_kernel, out_shape=jax.ShapeDtypeStruct((3, 3, span,...  3.63 us
    unnamed x4, local copies, waits for them, and re-layouts  2.68 us

profile of v4, /device:TPU:0, one launch (start us, length us, event | category | flops | bytes accessed | tf_op | source)
XLA Modules:
  0.0 84.2 jit_solution(17297469043395471197)
XLA Ops:
  0.7 0.8 fusion.7
  1.5 0.1 select_reduce_fusion
  1.6 0.1 copy.9
  1.7 0.6 reshape.26.place_ref
  2.3 0.6 sub.45.slot_ref
  2.9 0.1 reshape.29
  3.0 0.1 broadcast_in_dim.15
  3.1 0.1 reshape.27
  3.2 3.6 %shard_map.41.dense = bf16[3,3,256,256]{3,2,1,0:T(8,128)(2,1)} custom-call(s32[144]{0:T(256)} %sub.45.slot_ref, bf16[4,64,1152]{2,1,0:T(8,128)(2,1)} %v_ref.3), custom_call_target="tpu_custom_call" | custom-call | tf_op jit(solution)/shard_map/pallas_call | solution.py:324
  6.9 0.0 copy-start
  6.9 1.3 %copy-done = bf16[3,3,256,256]{3,2,1,0:T(8,128)(2,1)S(1)} copy-done((bf16[3,3,256,256]{3,2,1,0:T(8,128)(2,1)S(1)}, bf16[3,3,256,256]{3,2,1,0:T(8,128)(2,1)}, u32[]{:S(2)}) %copy-start) | copy-done | bytes 1179672
  8.1 68.4 %shard_map.42 = (f32[18,256,128]{2,1,0:T(8,128)S(1)}, f32[8,128]{1,0:T(8,128)S(1)}) custom-call(f32[9,4,256]{2,1,0:T(4,128)S(1)} %bitcast.4, bf16[3,3,256,256]{3,2,1,0:T(8,128)(2,1)S(1)} %copy-done), custom_call_target="tpu_custom_call" | custom-call | tf_op jit(solution)/shard_map/pallas_call | solution.py:330
  76.5 0.0 copy-start.1
  76.5 1.4 %copy-done.1 = f32[18,256,128]{2,1,0:T(8,128)} copy-done((f32[18,256,128]{2,1,0:T(8,128)}, f32[18,256,128]{2,1,0:T(8,128)S(1)}, u32[]{:S(2)}) %copy-start.1) | copy-done | bytes 2359320
  77.9 0.6 reduce_sum.19
  79.2 3.9 %shard_map.43 = bf16[4,64,1152]{2,1,0:T(8,128)(2,1)} custom-call(s32[72]{0:T(128)} %reshape.26.place_ref, f32[18,256,128]{2,1,0:T(8,128)} %copy-done.1, bf16[4,64,1152]{2,1,0:T(8,128)(2,1)} %v_ref.3), custom_call_target="tpu_custom_call" | custom-call | tf_op jit(solution)/shard_map/pallas_call | solution.py:357
  (4 shorter events, 0.0 us)
Async XLA Ops:
  6.9 1.3 %copy-start = (bf16[3,3,256,256]{3,2,1,0:T(8,128)(2,1)S(1)}, bf16[3,3,256,256]{3,2,1,0:T(8,128)(2,1)}, u32[]{:S(2)}) copy-start(bf16[3,3,256,256]{3,2,1,0:T(8,128)(2,1)} %shard_map.41.dense) | copy-start | bytes 3538948
  76.5 1.4 %copy-start.1 = (f32[18,256,128]{2,1,0:T(8,128)}, f32[18,256,128]{2,1,0:T(8,128)S(1)}, u32[]{:S(2)}) copy-start(f32[18,256,128]{2,1,0:T(8,128)S(1)} %get-tuple-element.4.total) | copy-start | bytes 7077892

commit v5 on v4

--- a/solution.py
+++ b/solution.py
@@ -27,7 +27,7 @@
     slot_at = jnp.sum(jnp.where(matches, slots, 0), axis=2) - 1
     stored = (slot_at >= 0).astype(jnp.float32)
     mask = jnp.repeat(stored.reshape(row_count, 9, row_count), block_size, axis=2)
-    return place.reshape(-1), slot_at.reshape(-1), mask.transpose(1, 0, 2)
+    return place, slot_at, mask.transpose(1, 0, 2)
 
 
 def swapped(tile):
@@ -40,7 +40,6 @@
 
 def expand_kernel(slot_ref, v_ref, dense):
     row_count, block, width = v_ref.shape
-    places = 9 * row_count
     pair = 2 * block
     low = low_half(block)
 
@@ -50,7 +49,10 @@
             for h in range(row_count // 2):
                 parts = []
                 for side in range(2):
-                    slot = slot_ref[x * places + c * row_count + 2 * h + side]
+                    if 2 * h + side == (x + 2) % row_count:
+                        parts.append(jnp.zeros((block, pair), jnp.float32))
+                        continue
+                    slot = slot_ref[x, c * row_count + 2 * h + side]
                     known = jnp.maximum(slot, 0)
                     at = pl.multiple_of((known >> 1) * pair, pair)
                     tile = v_ref[x, :, pl.ds(at, pair)].astype(jnp.float32)
@@ -60,10 +62,10 @@
                 dense[c // 3, c % 3, rows, pl.ds(h * pair, pair)] = both.astype(jnp.bfloat16)
         return carry
 
-    lax.fori_loop(0, 9, expand, 0)
-
-
-def compact_kernel(place_ref, total, v_ref, out_ref):
+    lax.fori_loop(0, 9, expand, 0, unroll=3)
+
+
+def compact_kernel(total_rows, place_ref, total, squares, v_ref, out_ref, mean_ref):
     row_count, block, width = v_ref.shape
     slot_count = width // block
     pair = 2 * block
@@ -75,7 +77,7 @@
             rows = pl.ds(x * block, block)
             parts = []
             for side in range(2):
-                place = place_ref[x * slot_count + 2 * k + side]
+                place = place_ref[x, 2 * k + side]
                 tile = total[place >> 1, rows, :]
                 parts.append(jnp.where((place & 1) == side, tile, swapped(tile)))
             both = jnp.where(low, parts[0], parts[1])
@@ -83,7 +85,9 @@
             out_ref[x, :, pl.ds(at, pair)] = (1.5 * own - 0.5 * both).astype(jnp.bfloat16)
         return carry
 
-    lax.fori_loop(0, slot_count // 2, compact, 0)
+    lax.fori_loop(0, slot_count // 2, compact, 0, unroll=3)
+    by_lane = jnp.sum(squares[...], axis=0, keepdims=True)
+    mean_ref[...] = jnp.sum(by_lane, axis=1, keepdims=True) / total_rows
 
 
 def kernel(lines_per_layer, device_count, mask_ref, dense, total, res_ref,
@@ -354,13 +358,15 @@
             collective_id=0, has_side_effects=True, vmem_limit_bytes=40 * 1024 * 1024
         ),
     )(mask, dense)
-    updated = pl.pallas_call(
-        compact_kernel,
-        out_shape=jax.ShapeDtypeStruct(values.shape, jnp.bfloat16),
-        in_specs=[smem, vmem, vmem],
-        out_specs=vmem,
-    )(place, total, values)
-    residual = jnp.sum(squares) / (total_rows * block_size)
+    updated, residual = pl.pallas_call(
+        functools.partial(compact_kernel, total_rows * block_size),
+        out_shape=(
+            jax.ShapeDtypeStruct(values.shape, jnp.bfloat16),
+            jax.ShapeDtypeStruct((1, 1), jnp.float32),
+        ),
+        in_specs=[smem, vmem, vmem, vmem],
+        out_specs=(vmem, vmem),
+    )(place, total, squares, values)
     return (updated, residual.reshape(1))
 
 

time: 84.8 us -> 81.5 us (0.961)
  between operations: 2.49 us -> 0.72 us
  Pallas kernels: 75.9 us -> 75 us
    unnamed x4 -> x11, local copies, waits for them, and re-layouts: 2.68 us -> 4.04 us
where the time goes in v5:
time: 81.5 us; the launch traced here: 80.9 us
  Pallas kernels  75 us (92%)
  local copies, waits for them, and re-layouts  4.5 us (6%)
    pallas_call x1, Pallas kernels, on_device(): pl.pallas_call(functools.partial(kernel, lines_per_layer, device_count),...  68.4 us
    unnamed x11, local copies, waits for them, and re-layouts  4.04 us
    pallas_call x1, Pallas kernels, on_device(): pl.pallas_call(functools.partial(compact_kernel, total_rows * block_size)...  3.45 us
    pallas_call x1, Pallas kernels, on_device(): pl.pallas_call(expand_kernel, out_shape=jax.ShapeDtypeStruct((3, 3, span,...  3.14 us

profile of v5, /device:TPU:0, one launch (start us, length us, event | category | flops | bytes accessed | tf_op | source)
XLA Modules:
  0.0 80.9 jit_solution(8458516144778663407)
XLA Ops:
  0.6 0.0 copy-start
  0.7 0.7 copy-done
  1.3 0.1 constant_dynamic-slice_fusion
  1.4 0.1 copy.11
  1.5 0.0 copy-start.4
  1.6 0.1 copy.9
  1.6 0.1 select_reduce_fusion
  1.8 0.6 broadcast_add_fusion.slot_ref
  2.4 0.1 reshape.21
  2.5 0.1 broadcast_in_dim.15
  2.5 0.1 reshape.19
  2.7 3.1 %shard_map.41.dense = bf16[3,3,256,256]{3,2,1,0:T(8,128)(2,1)} custom-call(s32[4,36]{1,0:T(4,128)} %broadcast_add_fusion.slot_ref, bf16[4,64,1152]{2,1,0:T(8,128)(2,1)} %v_ref.3), custom_call_target="tpu_custom_call" | custom-call | tf_op jit(solution)/shard_map/pallas_call | solution.py:328
  5.8 0.0 copy-start.1
  5.8 1.3 %copy-done.1 = bf16[3,3,256,256]{3,2,1,0:T(8,128)(2,1)S(1)} copy-done((bf16[3,3,256,256]{3,2,1,0:T(8,128)(2,1)S(1)}, bf16[3,3,256,256]{3,2,1,0:T(8,128)(2,1)}, u32[]{:S(2)}) %copy-start.1) | copy-done | bytes 1179672
  7.1 68.4 %shard_map.42 = (f32[18,256,128]{2,1,0:T(8,128)S(1)}, f32[8,128]{1,0:T(8,128)S(1)}) custom-call(f32[9,4,256]{2,1,0:T(4,128)S(1)} %bitcast.4, bf16[3,3,256,256]{3,2,1,0:T(8,128)(2,1)S(1)} %copy-done.1), custom_call_target="tpu_custom_call" | custom-call | tf_op jit(solution)/shard_map/pallas_call | solution.py:334
  75.5 0.0 copy-start.2
  75.5 1.4 %copy-done.2 = f32[18,256,128]{2,1,0:T(8,128)} copy-done((f32[18,256,128]{2,1,0:T(8,128)}, f32[18,256,128]{2,1,0:T(8,128)S(1)}, u32[]{:S(2)}) %copy-start.2) | copy-done | bytes 2359320
  76.9 0.0 copy-start.3
  76.9 0.6 copy-done.3
  77.5 0.0 copy-done.4
  77.5 3.4 %shard_map.43 = (bf16[4,64,1152]{2,1,0:T(8,128)(2,1)}, f32[1,1]{1,0:T(1,128)}) custom-call(s32[4,18]{1,0:T(4,128)} %copy-done.4, f32[18,256,128]{2,1,0:T(8,128)} %copy-done.2, f32[8,128]{1,0:T(8,128)} %copy-done.3, bf16[4,64,1152]{2,1,0:T(8,128)(2,1)} %v_ref.3), custom_call_target="tpu_custom_call" | custom-call | tf_op jit(solution)/shard_map/pallas_call | solution.py:361
  (4 shorter events, 0.1 us)
Async XLA Ops:
  0.6 0.7 copy-start
  1.5 75.9 %copy-start.4 = (s32[4,18]{1,0:T(4,128)}, s32[4,18]{1,0:T(4,128)S(1)}, u32[]{:S(2)}) copy-start(s32[4,18]{1,0:T(4,128)S(1)} %fusion.7.place_ref) | copy-start | bytes 868
  5.8 1.3 %copy-start.1 = (bf16[3,3,256,256]{3,2,1,0:T(8,128)(2,1)S(1)}, bf16[3,3,256,256]{3,2,1,0:T(8,128)(2,1)}, u32[]{:S(2)}) copy-start(bf16[3,3,256,256]{3,2,1,0:T(8,128)(2,1)} %shard_map.41.dense) | copy-start | bytes 3538948
  75.5 1.4 %copy-start.2 = (f32[18,256,128]{2,1,0:T(8,128)}, f32[18,256,128]{2,1,0:T(8,128)S(1)}, u32[]{:S(2)}) copy-start(f32[18,256,128]{2,1,0:T(8,128)S(1)} %get-tuple-element.6.total) | copy-start | bytes 7077892
  76.9 0.6 copy-start.3

commit v6 on v5

--- a/solution.py
+++ b/solution.py
@@ -168,25 +168,26 @@
         for o in range(1, LAYERS):
             bank_z(o).start()
 
-    def z_copy(phase, d, j):
+    def z_copy(phase, d, j, ky):
         plane = 1 if j == 0 else 2 * (1 - d)
-        return remote(packed.at[phase, plane], zbuf.at[phase, d, j],
-                      zsend.at[phase, d, j], zrecv.at[phase, d, j], z_to[d])
+        return remote(packed.at[phase, plane, ky], zbuf.at[phase, d, j, ky],
+                      zsend.at[phase, d, j, ky], zrecv.at[phase, d, j, ky], z_to[d])
 
     def y_copy(phase, d, plane):
         return remote(packed.at[phase, plane, pl.ds(1 - d, 2)], ybuf.at[phase, d, plane],
                       ysend.at[phase, d, plane], yrecv.at[phase, d, plane], y_to[d])
 
-    def g_copy(phase, zd, yd, j):
-        return remote(zbuf.at[phase, zd, j, pl.ds(1 - yd, 2)], gbuf.at[phase, zd, yd, j],
-                      gsend.at[phase, zd, yd, j], grecv.at[phase, zd, yd, j], y_to[yd])
+    def g_copy(phase, zd, yd, j, i):
+        return remote(zbuf.at[phase, zd, j, 1 - yd + i], gbuf.at[phase, zd, yd, j, i],
+                      gsend.at[phase, zd, yd, j, i], grecv.at[phase, zd, yd, j, i], y_to[yd])
 
     def place_of(d, j):
         return 2 * d if j == 0 else 1
 
     def send_z(phase, j):
-        for d in range(2):
-            z_copy(phase, d, j).start()
+        for ky in (1, 0, 2):
+            for d in range(2):
+                z_copy(phase, d, j, ky).start()
 
     def send_y(phase, planes):
         for plane in planes:
@@ -194,10 +195,12 @@
                 y_copy(phase, d, plane).start()
 
     def relay(phase, j):
-        for zd in range(2):
-            z_copy(phase, zd, j).wait_recv()
-            for yd in range(2):
-                g_copy(phase, zd, yd, j).start()
+        for ky in (1, 0, 2):
+            for zd in range(2):
+                z_copy(phase, zd, j, ky).wait_recv()
+                for yd in range(2):
+                    if 0 <= ky - 1 + yd <= 1:
+                        g_copy(phase, zd, yd, j, ky - 1 + yd).start()
 
     def accumulate(mz, my, source, nz, ny, z0, y0, first=False):
         def step(i, carry):
@@ -232,7 +235,8 @@
     def add_g(phase, j):
         for zd in range(2):
             for yd in range(2):
-                g_copy(phase, zd, yd, j).wait_recv()
+                for i in range(2):
+                    g_copy(phase, zd, yd, j, i).wait_recv()
                 accumulate(2 * zd, 2 * yd, lambda kz, ky: gbuf.at[phase, zd, yd, j, ky],
                            1, 2, place_of(zd, j), yd)
 
@@ -303,9 +307,11 @@
             for plane in range(3):
                 y_copy(phase, d, plane).wait_send()
             for j in range(2):
-                z_copy(phase, d, j).wait_send()
+                for ky in range(3):
+                    z_copy(phase, d, j, ky).wait_send()
                 for yd in range(2):
-                    g_copy(phase, d, yd, j).wait_send()
+                    for i in range(2):
+                        g_copy(phase, d, yd, j, i).wait_send()
     for o in range(1, lines_per_layer):
         bank_y(o).wait_send()
     for o in range(1, LAYERS):
@@ -344,12 +350,12 @@
             pltpu.VMEM((2, 2, 2, 3, pieces, pair), jnp.bfloat16),
             pltpu.VMEM((2, 2, 3, 2, pieces, pair), jnp.bfloat16),
             pltpu.VMEM((2, 2, 2, 2, 2, pieces, pair), jnp.bfloat16),
-            dma((2, 2, 2)),
-            dma((2, 2, 2)),
+            dma((2, 2, 2, 3)),
+            dma((2, 2, 2, 3)),
             dma((2, 2, 3)),
             dma((2, 2, 3)),
-            dma((2, 2, 2, 2)),
-            dma((2, 2, 2, 2)),
+            dma((2, 2, 2, 2, 2)),
+            dma((2, 2, 2, 2, 2)),
             pltpu.VMEM((lines_per_layer + LAYERS, 8, pair), jnp.float32),
             dma((lines_per_layer + LAYERS - 2,)),
             dma((lines_per_layer + LAYERS - 2,)),

time: 81.5 us -> 83.2 us (1.021)
  Pallas kernels: 75 us -> 77 us
    pallas_call x1, Pallas kernels: 68.4 us -> 70.4 us  [on_device(): pl.pallas_call(functools.partial(kernel, lines_per_layer, device_count),...]
where the time goes in v6:
time: 83.2 us; the launch traced here: 82.9 us
  Pallas kernels  77 us (93%)
  local copies, waits for them, and re-layouts  4.5 us (5%)
    pallas_call x1, Pallas kernels, on_device(): pl.pallas_call(functools.partial(kernel, lines_per_layer, device_count),...  70.4 us
    unnamed x11, local copies, waits for them, and re-layouts  4.04 us
    pallas_call x1, Pallas kernels, on_device(): pl.pallas_call(functools.partial(compact_kernel, total_rows * block_size)...  3.45 us
    pallas_call x1, Pallas kernels, on_device(): pl.pallas_call(expand_kernel, out_shape=jax.ShapeDtypeStruct((3, 3, span,...  3.14 us

profile of v6, /device:TPU:0, one launch (start us, length us, event | category | flops | bytes accessed | tf_op | source)
XLA Modules:
  0.0 82.9 jit_solution(17615297770173113908)
XLA Ops:
  0.6 0.0 copy-start
  0.7 0.7 copy-done
  1.3 0.1 constant_dynamic-slice_fusion
  1.4 0.1 copy.11
  1.5 0.0 copy-start.4
  1.6 0.1 copy.9
  1.6 0.1 select_reduce_fusion
  1.8 0.6 broadcast_add_fusion.slot_ref
  2.4 0.1 reshape.21
  2.5 0.1 broadcast_in_dim.15
  2.5 0.1 reshape.19
  2.7 3.1 %shard_map.41.dense = bf16[3,3,256,256]{3,2,1,0:T(8,128)(2,1)} custom-call(s32[4,36]{1,0:T(4,128)} %broadcast_add_fusion.slot_ref, bf16[4,64,1152]{2,1,0:T(8,128)(2,1)} %v_ref.3), custom_call_target="tpu_custom_call" | custom-call | tf_op jit(solution)/shard_map/pallas_call | solution.py:334
  5.8 0.0 copy-start.1
  5.8 1.3 %copy-done.1 = bf16[3,3,256,256]{3,2,1,0:T(8,128)(2,1)S(1)} copy-done((bf16[3,3,256,256]{3,2,1,0:T(8,128)(2,1)S(1)}, bf16[3,3,256,256]{3,2,1,0:T(8,128)(2,1)}, u32[]{:S(2)}) %copy-start.1) | copy-done | bytes 1179672
  7.1 70.4 %shard_map.42 = (f32[18,256,128]{2,1,0:T(8,128)S(1)}, f32[8,128]{1,0:T(8,128)S(1)}) custom-call(f32[9,4,256]{2,1,0:T(4,128)S(1)} %bitcast.4, bf16[3,3,256,256]{3,2,1,0:T(8,128)(2,1)S(1)} %copy-done.1), custom_call_target="tpu_custom_call" | custom-call | tf_op jit(solution)/shard_map/pallas_call | solution.py:340
  77.5 0.0 copy-start.2
  77.5 1.4 %copy-done.2 = f32[18,256,128]{2,1,0:T(8,128)} copy-done((f32[18,256,128]{2,1,0:T(8,128)}, f32[18,256,128]{2,1,0:T(8,128)S(1)}, u32[]{:S(2)}) %copy-start.2) | copy-done | bytes 2359320
  78.9 0.0 copy-start.3
  78.9 0.6 copy-done.3
  79.5 0.0 copy-done.4
  79.5 3.4 %shard_map.43 = (bf16[4,64,1152]{2,1,0:T(8,128)(2,1)}, f32[1,1]{1,0:T(1,128)}) custom-call(s32[4,18]{1,0:T(4,128)} %copy-done.4, f32[18,256,128]{2,1,0:T(8,128)} %copy-done.2, f32[8,128]{1,0:T(8,128)} %copy-done.3, bf16[4,64,1152]{2,1,0:T(8,128)(2,1)} %v_ref.3), custom_call_target="tpu_custom_call" | custom-call | tf_op jit(solution)/shard_map/pallas_call | solution.py:367
  (4 shorter events, 0.1 us)
Async XLA Ops:
  0.6 0.7 copy-start
  1.5 77.9 %copy-start.4 = (s32[4,18]{1,0:T(4,128)}, s32[4,18]{1,0:T(4,128)S(1)}, u32[]{:S(2)}) copy-start(s32[4,18]{1,0:T(4,128)S(1)} %fusion.7.place_ref) | copy-start | bytes 868
  5.8 1.3 %copy-start.1 = (bf16[3,3,256,256]{3,2,1,0:T(8,128)(2,1)S(1)}, bf16[3,3,256,256]{3,2,1,0:T(8,128)(2,1)}, u32[]{:S(2)}) copy-start(bf16[3,3,256,256]{3,2,1,0:T(8,128)(2,1)} %shard_map.41.dense) | copy-start | bytes 3538948
  77.5 1.4 %copy-start.2 = (f32[18,256,128]{2,1,0:T(8,128)}, f32[18,256,128]{2,1,0:T(8,128)S(1)}, u32[]{:S(2)}) copy-start(f32[18,256,128]{2,1,0:T(8,128)S(1)} %get-tuple-element.6.total) | copy-start | bytes 7077892
  78.9 0.6 copy-start.3

commit v7 on v5

--- a/solution.py
+++ b/solution.py
@@ -273,10 +273,10 @@
     relay(0, 0)
     add_y(0)
     add_z(0, 0)
+    relay(0, 1)
     add_g(0, 0)
     outer = to_square(0) + to_square(2)
     send_z(1, 1)
-    relay(0, 1)
     send_y(1, (0, 2))
     add_z(0, 1)
     add_g(0, 1)

time: 81.5 us -> 80.3 us (0.985)
  Pallas kernels: 75 us -> 73.5 us
    pallas_call x1, Pallas kernels: 68.4 us -> 66.9 us  [on_device(): pl.pallas_call(functools.partial(kernel, lines_per_layer, device_count),...]
where the time goes in v7:
time: 80.3 us; the launch traced here: 79.4 us
  Pallas kernels  73.5 us (92%)
  local copies, waits for them, and re-layouts  4.5 us (6%)
    pallas_call x1, Pallas kernels, on_device(): pl.pallas_call(functools.partial(kernel, lines_per_layer, device_count),...  66.9 us
    unnamed x11, local copies, waits for them, and re-layouts  4.04 us
    pallas_call x1, Pallas kernels, on_device(): pl.pallas_call(functools.partial(compact_kernel, total_rows * block_size)...  3.45 us
    pallas_call x1, Pallas kernels, on_device(): pl.pallas_call(expand_kernel, out_shape=jax.ShapeDtypeStruct((3, 3, span,...  3.14 us

profile of v7, /device:TPU:0, one launch (start us, length us, event | category | flops | bytes accessed | tf_op | source)
XLA Modules:
  0.0 79.4 jit_solution(14417772631645950046)
XLA Ops:
  0.6 0.0 copy-start
  0.7 0.7 copy-done
  1.3 0.1 constant_dynamic-slice_fusion
  1.4 0.1 copy.11
  1.5 0.0 copy-start.4
  1.6 0.1 copy.9
  1.6 0.1 select_reduce_fusion
  1.8 0.6 broadcast_add_fusion.slot_ref
  2.4 0.1 reshape.21
  2.5 0.1 broadcast_in_dim.15
  2.5 0.1 reshape.19
  2.7 3.1 %shard_map.41.dense = bf16[3,3,256,256]{3,2,1,0:T(8,128)(2,1)} custom-call(s32[4,36]{1,0:T(4,128)} %broadcast_add_fusion.slot_ref, bf16[4,64,1152]{2,1,0:T(8,128)(2,1)} %v_ref.3), custom_call_target="tpu_custom_call" | custom-call | tf_op jit(solution)/shard_map/pallas_call | solution.py:328
  5.8 0.0 copy-start.1
  5.8 1.3 %copy-done.1 = bf16[3,3,256,256]{3,2,1,0:T(8,128)(2,1)S(1)} copy-done((bf16[3,3,256,256]{3,2,1,0:T(8,128)(2,1)S(1)}, bf16[3,3,256,256]{3,2,1,0:T(8,128)(2,1)}, u32[]{:S(2)}) %copy-start.1) | copy-done | bytes 1179672
  7.1 66.9 %shard_map.42 = (f32[18,256,128]{2,1,0:T(8,128)S(1)}, f32[8,128]{1,0:T(8,128)S(1)}) custom-call(f32[9,4,256]{2,1,0:T(4,128)S(1)} %bitcast.4, bf16[3,3,256,256]{3,2,1,0:T(8,128)(2,1)S(1)} %copy-done.1), custom_call_target="tpu_custom_call" | custom-call | tf_op jit(solution)/shard_map/pallas_call | solution.py:334
  74.0 0.0 copy-start.2
  74.0 1.4 %copy-done.2 = f32[18,256,128]{2,1,0:T(8,128)} copy-done((f32[18,256,128]{2,1,0:T(8,128)}, f32[18,256,128]{2,1,0:T(8,128)S(1)}, u32[]{:S(2)}) %copy-start.2) | copy-done | bytes 2359320
  75.4 0.0 copy-start.3
  75.4 0.6 copy-done.3
  76.0 0.0 copy-done.4
  76.0 3.4 %shard_map.43 = (bf16[4,64,1152]{2,1,0:T(8,128)(2,1)}, f32[1,1]{1,0:T(1,128)}) custom-call(s32[4,18]{1,0:T(4,128)} %copy-done.4, f32[18,256,128]{2,1,0:T(8,128)} %copy-done.2, f32[8,128]{1,0:T(8,128)} %copy-done.3, bf16[4,64,1152]{2,1,0:T(8,128)(2,1)} %v_ref.3), custom_call_target="tpu_custom_call" | custom-call | tf_op jit(solution)/shard_map/pallas_call | solution.py:361
  (4 shorter events, 0.1 us)
Async XLA Ops:
  0.6 0.7 copy-start
  1.5 74.4 %copy-start.4 = (s32[4,18]{1,0:T(4,128)}, s32[4,18]{1,0:T(4,128)S(1)}, u32[]{:S(2)}) copy-start(s32[4,18]{1,0:T(4,128)S(1)} %fusion.7.place_ref) | copy-start | bytes 868
  5.8 1.3 %copy-start.1 = (bf16[3,3,256,256]{3,2,1,0:T(8,128)(2,1)S(1)}, bf16[3,3,256,256]{3,2,1,0:T(8,128)(2,1)}, u32[]{:S(2)}) copy-start(bf16[3,3,256,256]{3,2,1,0:T(8,128)(2,1)} %shard_map.41.dense) | copy-start | bytes 3538948
  74.0 1.4 %copy-start.2 = (f32[18,256,128]{2,1,0:T(8,128)}, f32[18,256,128]{2,1,0:T(8,128)S(1)}, u32[]{:S(2)}) copy-start(f32[18,256,128]{2,1,0:T(8,128)S(1)} %get-tuple-element.6.total) | copy-start | bytes 7077892
  75.4 0.6 copy-start.3
